TPU v7x, 32 devices: a whole 2x2x4 slice. The times are simulated.
32 devices in a mesh: dp: 16 (over z, x, core), tensor: 2 (over y).
Axes of the slice: x: 2, y: 2, z: 4, core: 2. Of those that a mesh axis runs over, the one named last changes fastest.
Arguments:
- features: bfloat16 [8192, 1280], P('dp'), may hold values from -6 to 6
- class_bias: float32 [1536], P('tensor')
- logits: bfloat16 [8192, 1536], P('dp', 'tensor'), may hold values from -12 to 12
- tile_lists: int32 [256, 2], P('dp'), may hold values from 0 to 15, all different within a row; in each aligned block of 16 rows (0 to 15, 16 to 31, ...) at most 4 rows name the same one
- valid_counts: int32 [16], P('dp'), may hold values from 192 to 512, as said below
Outputs:
- log_labels: float32 [8192, 1536], P('dp', 'tensor')
Inputs may be any that keep to these rules, and one draw needn't show every extreme that they name: `tile_lists`: each row names 2 different tiles; among the 16 rows of one index of dp no tile is named more than 4 times. `valid_counts`: some tile is fully valid.
All inputs are finite; a program needn't handle non-finite values.
Results may differ from a plain program's by a relative error of at most 0.0005.
Values may be sent and summed in bfloat16 or wider, within the bound.
A program may use at most 128 MiB of HBM per device.

v0:
```python
import math

import jax
import jax.numpy as jnp
from jax import lax
from jax.sharding import PartitionSpec as P

SWEEPS = 2


ALPHA = 0.75
SOFTMAX_TEMPER = 0.05
EPSILON = 1e-06


def unitnorm_rows(features):
    wide = features.astype(jnp.float32)
    scale = lax.rsqrt(jnp.mean(wide * wide, axis=1, keepdims=True) + EPSILON)
    return (wide * scale / math.sqrt(wide.shape[1])).astype(jnp.bfloat16)


def on_device(features, class_bias, logits, tile_lists, valid_counts):
    adjusted = logits.astype(jnp.float32) + class_bias[None, :]
    exponentials = jnp.exp(adjusted)
    row_totals = lax.psum(jnp.sum(exponentials, axis=1), "tensor")
    prior = (exponentials / row_totals[:, None]).astype(jnp.bfloat16)
    normalized = unitnorm_rows(features)
    devices = lax.axis_size("dp")
    capacity = max(2, 64 // devices)
    slot_count = devices * capacity
    block_count, tile_count = tile_lists.shape
    block_rows = normalized.shape[0] // block_count
    feature_width = normalized.shape[1]
    owners = tile_lists.reshape(-1)
    requests = owners.shape[0]
    owner_hits = (owners[:, None] == jnp.arange(devices, dtype=jnp.int32)[None, :]).astype(
        jnp.int32
    )
    earlier = jnp.sum((jnp.cumsum(owner_hits, axis=0) - owner_hits) * owner_hits, axis=1)
    position = owners * capacity + earlier
    matches = position[None, :] == jnp.arange(slot_count, dtype=jnp.int32)[:, None]
    filled = jnp.any(matches, axis=1)
    source = jnp.sum(jnp.where(matches, jnp.arange(requests, dtype=jnp.int32)[None, :], 0), axis=1)
    query_blocks = normalized.reshape(block_count, block_rows, feature_width)
    outgoing = jnp.where(
        filled[:, None, None], query_blocks[source // tile_count], jnp.zeros((), jnp.bfloat16)
    )
    outgoing = outgoing.reshape(devices, capacity, block_rows, feature_width)
    arrived = lax.all_to_all(outgoing, "dp", split_axis=0, concat_axis=0, tiled=True)
    affinity_scores = (
        jnp.einsum("scqd,md->scqm", arrived, normalized, preferred_element_type=jnp.float32)
        / SOFTMAX_TEMPER
    )
    columns = jnp.arange(normalized.shape[0], dtype=jnp.int32)
    weights = jnp.where(columns < valid_counts[0], jnp.exp(affinity_scores), 0.0).astype(
        jnp.bfloat16
    )
    tile_sums = jnp.sum(weights.astype(jnp.float32), axis=3)
    returned_sums = lax.all_to_all(tile_sums, "dp", split_axis=0, concat_axis=0, tiled=True)
    picked_sums = returned_sums.reshape(slot_count, block_rows)[position]
    denominator = jnp.sum(picked_sums.reshape(block_count, tile_count, block_rows), axis=1).reshape(
        -1
    )
    prior_float = prior.astype(jnp.float32)
    label_matrix = prior
    spread = prior_float
    for sweep_index in range(SWEEPS):
        partial_sums = jnp.einsum(
            "scqm,mk->scqk", weights, label_matrix, preferred_element_type=jnp.float32
        ).astype(jnp.bfloat16)
        returned = lax.all_to_all(partial_sums, "dp", split_axis=0, concat_axis=0, tiled=True)
        picked = returned.reshape(slot_count, block_rows, -1)[position].astype(jnp.float32)
        numerator = jnp.sum(picked.reshape(block_count, tile_count, block_rows, -1), axis=1)
        numerator = numerator.reshape(denominator.shape[0], -1)
        spread = ALPHA * numerator / denominator[:, None] + (1.0 - ALPHA) * prior_float
        label_matrix = spread.astype(jnp.bfloat16)
    return jnp.log(spread)


def solution(mesh):
    in_specs = (P("dp", None), P("tensor"), P("dp", "tensor"), P("dp", None), P("dp"))
    out_specs = P("dp", "tensor")
    return jax.shard_map(
        on_device, mesh=mesh, in_specs=in_specs, out_specs=out_specs, check_vma=False
    )
```

profile of v0, /device:TPU:1, one launch (start us, length us, event | category | flops | bytes accessed | tf_op | source)
XLA Modules:
  0.0 317.7 jit_solution(12125010477296436905)
XLA Ops:
  0.0 0.9 copy.10
  0.9 0.1 reshape.143
  1.0 0.1 fusion.12
  1.0 0.1 reduce_window_sum.11
  1.1 0.2 select_reduce_fusion.1
  1.3 0.1 select_reduce_fusion
  1.4 0.1 fusion.11
  1.5 1.6 fusion
  3.2 0.0 copy-done.3
  3.2 0.4 fusion.2
  3.5 0.1 broadcast_in_dim.47
  3.6 3.2 %gather_fusion = bf16[64,32,1280]{2,1,0:T(8,128)(2,1)} fusion(bf16[16,32,1280]{2,1,0:T(8,128)(2,1)S(1)} %bitcast.64, s32[1024]{0:T(1024)S(1)} %pad_clamp_fusion.1), kind=kCustom, calls=%fused_computation | custom fusion | bytes 10486016 | tf_op jit(solution)/shard_map/gather | solution.py:46
  6.8 5.2 %broadcast_select_fusion = bf16[16,4,32,1280]{3,2,1,0:T(8,128)(2,1)} fusion(bf16[16,4,32,1280]{3,2,1,0:T(8,128)(2,1)} %bitcast.65, pred[16,4]{1,0:T(8,128)(4,1)S(1)} %broadcast_in_dim.47), kind=kLoop, calls=%fused_computation.4 | loop fusion | flops 2621440 | bytes 10485824 | tf_op jit(solution)/shard_map/jit(_where)/select_n | solution.py:45
  12.1 7.5 %all-to-all-start = ((bf16[16,4,32,1280]{3,2,1,0:T(8,128)(2,1)}), bf16[16,4,32,1280]{3,2,1,0:T(8,128)(2,1)}, u32[]{:S(2)}, u32[]{:S(2)}) async-start(bf16[16,4,32,1280]{3,2,1,0:T(8,128)(2,1)} %broadcast_select_fusion), calls=%async_computation | async-start | bytes 10485760 | tf_op jit(solution)/shard_map/all_to_all | solution.py:49
  20.2 0.0 copy-done
  20.2 0.3 fusion.7
  20.5 4.2 %psum.7 = f32[512]{0:T(512)S(1)} all-reduce(f32[512]{0:T(512)S(1)} %fusion.7), channel_id=1, replica_groups=mesh['dp'=16,'tensor'=2] {'tensor'}, use_global_device_ids=true, to_apply=%region_6.7 | all-reduce | flops 512 | bytes 4096 | tf_op jit(solution)/shard_map/psum | solution.py:25
  24.7 91.1 %all-to-all-done = bf16[16,4,32,1280]{3,2,1,0:T(8,128)(2,1)} async-done(((bf16[16,4,32,1280]{3,2,1,0:T(8,128)(2,1)}), bf16[16,4,32,1280]{3,2,1,0:T(8,128)(2,1)}, u32[]{:S(2)}, u32[]{:S(2)}) %all-to-all-start) | async-done | bytes 5242912 | tf_op jit(solution)/shard_map/all_to_all | solution.py:49
  115.9 6.7 %convert_reduce_fusion = (f32[16,4,32]{2,1,0:T(4,128)S(1)}, bf16[16,4,32,512]{3,2,1,0:T(8,128)(2,1)}) fusion(bf16[16,4,32,1280]{3,2,1,0:T(8,128)(2,1)} %all-to-all-done, bf16[512,1280]{1,0:T(8,128)(2,1)S(1)} %fusion.2, pred[512]{0:T(512)(128)(4,1)S(1)} %iota_compare_fusion.2), kind=kOutput, calls=%fused_computation.5 | convolution fusion | flops 2689595392 | bytes 8659456 | tf_op jit(solution)/shard_map/scqd,md->scqm/dot_general | solution.py:51
  122.6 0.7 reshape.186
  123.3 23.5 %all-to-all-start.2 = ((f32[16,1,128]{2,1,0:T(1,128)}), f32[16,1,128]{2,1,0:T(1,128)S(1)}, u32[]{:S(2)}, u32[]{:S(2)}) async-start(f32[16,1,128]{2,1,0:T(1,128)} %reshape.186), calls=%async_computation.2 | async-start | bytes 16384 | tf_op jit(solution)/shard_map/all_to_all | solution.py:59
  146.8 5.2 %convolution_convert_fusion.1 = bf16[16,4,32,768]{3,2,1,0:T(8,128)(2,1)} fusion(bf16[16,4,32,512]{3,2,1,0:T(8,128)(2,1)} %get-tuple-element.6, bf16[512,768]{1,0:T(8,128)(2,1)S(1)} %copy-done, f32[512]{0:T(512)S(1)} %psum.7, f32[768]{0:T(1024)S(1)} %copy-done.4), kind=kOutput, calls=%fused_computation.15 | convolution fusion | flops 1613758464 | bytes 6034432 | tf_op jit(solution)/shard_map/scqm,mk->scqk/dot_general | solution.py:68
  152.0 0.5 all-to-all-done.2
  152.5 5.6 %all-to-all-start.1 = ((bf16[16,4,32,768]{3,2,1,0:T(8,128)(2,1)}), bf16[16,4,32,768]{3,2,1,0:T(8,128)(2,1)S(1)}, u32[]{:S(2)}, u32[]{:S(2)}) async-start(bf16[16,4,32,768]{3,2,1,0:T(8,128)(2,1)} %convolution_convert_fusion.1), calls=%async_computation.1 | async-start | bytes 6291456 | tf_op jit(solution)/shard_map/all_to_all | solution.py:71
  158.2 0.0 copy-done.5
  158.2 0.1 copy.11
  158.3 0.1 mul.62
  158.4 0.5 broadcast.152
  158.9 0.7 reduce
  159.6 0.1 reshape.187
  159.6 0.6 gather_fusion.2
  160.2 0.1 div.63
  160.3 57.6 %all-to-all-done.1 = bf16[16,4,32,768]{3,2,1,0:T(8,128)(2,1)S(1)} async-done(((bf16[16,4,32,768]{3,2,1,0:T(8,128)(2,1)}), bf16[16,4,32,768]{3,2,1,0:T(8,128)(2,1)S(1)}, u32[]{:S(2)}, u32[]{:S(2)}) %all-to-all-start.1) | async-done | bytes 3145760 | tf_op jit(solution)/shard_map/all_to_all | solution.py:71
  217.9 1.8 gather_fusion.1
  219.7 1.9 convert_reduce_fusion.2
  221.5 0.0 copy-start.1
  221.5 0.1 broadcast_multiply_fusion.1
  221.7 1.0 copy-done.1
  222.7 0.5 fusion.6
  223.2 1.1 copy-done.6
  224.3 1.8 convolution_convert_fusion
  226.1 85.0 %all_to_all.20 = bf16[16,4,32,768]{3,2,1,0:T(8,128)(2,1)S(1)} all-to-all(bf16[16,4,32,768]{3,2,1,0:T(8,128)(2,1)S(1)} %convolution_convert_fusion), channel_id=1, replica_groups=mesh['dp'=16,'tensor'=2] {'dp'}, dimensions={0} | all-to-all | bytes 6291456 | tf_op jit(solution)/shard_map/all_to_all | solution.py:71
  311.1 1.8 gather_fusion.3
  312.9 1.9 convert_reduce_fusion.1
  314.7 0.0 copy-start.2
  314.8 0.1 broadcast_multiply_fusion
  314.9 1.0 copy-done.2
  315.9 1.8 fusion.4
  (15 shorter events, 0.1 us)
Async XLA Ops:
  0.0 3.2 copy-start.3
  12.1 8.1 %copy-start = (bf16[512,768]{1,0:T(8,128)(2,1)S(1)}, bf16[512,768]{1,0:T(8,128)(2,1)}, u32[]{:S(2)}) copy-start(bf16[512,768]{1,0:T(8,128)(2,1)} %param.7) | copy-start | bytes 2359300
  12.1 8.1 %copy-start.4 = (f32[768]{0:T(1024)S(1)}, f32[768]{0:T(1024)}, u32[]{:S(2)}) copy-start(f32[768]{0:T(1024)} %param.6) | copy-start | bytes 9220
  12.1 103.8 %all-to-all-start = ((bf16[16,4,32,1280]{3,2,1,0:T(8,128)(2,1)}), bf16[16,4,32,1280]{3,2,1,0:T(8,128)(2,1)}, u32[]{:S(2)}, u32[]{:S(2)}) async-start(bf16[16,4,32,1280]{3,2,1,0:T(8,128)(2,1)} %broadcast_select_fusion), calls=%async_computation | async-start | bytes 10485760 | tf_op jit(solution)/shard_map/all_to_all | solution.py:49
  123.3 29.2 %all-to-all-start.2 = ((f32[16,1,128]{2,1,0:T(1,128)}), f32[16,1,128]{2,1,0:T(1,128)S(1)}, u32[]{:S(2)}, u32[]{:S(2)}) async-start(f32[16,1,128]{2,1,0:T(1,128)} %reshape.186), calls=%async_computation.2 | async-start | bytes 16384 | tf_op jit(solution)/shard_map/all_to_all | solution.py:59
  152.0 6.2 %copy-start.5 = (s32[16,2]{0,1:T(2,128)S(1)}, s32[16,2]{0,1:T(2,128)}, u32[]{:S(2)}) copy-start(s32[16,2]{0,1:T(2,128)} %param.8) | copy-start | bytes 388
  152.5 65.3 %all-to-all-start.1 = ((bf16[16,4,32,768]{3,2,1,0:T(8,128)(2,1)}), bf16[16,4,32,768]{3,2,1,0:T(8,128)(2,1)S(1)}, u32[]{:S(2)}, u32[]{:S(2)}) async-start(bf16[16,4,32,768]{3,2,1,0:T(8,128)(2,1)} %convolution_convert_fusion.1), calls=%async_computation.1 | async-start | bytes 6291456 | tf_op jit(solution)/shard_map/all_to_all | solution.py:71
  221.5 1.1 copy-start.1
  222.7 1.6 copy-start.6
  314.7 1.1 copy-start.2
where the time goes:
time: 318 us
  waiting for transfers between devices  149 us (47%)
  blocking collectives  89.2 us (28%)
  starting transfers between devices  36.6 us (12%)
  other arithmetic  15.1 us (5%)
  matrix products  13.7 us (4%)
  local copies, waits for them, and re-layouts  13 us (4%)
    all_to_all x1, waiting for transfers between devices, on_device(): lax.all_to_all(outgoing, 'dp', split_axis=0, concat_axis=0, tiled=True)  91.1 us
    all_to_all x1, blocking collectives, on_device(): lax.all_to_all(partial_sums, 'dp', split_axis=0, concat_axis=0, tiled=True)  85 us
    all_to_all x1, waiting for transfers between devices, on_device(): lax.all_to_all(partial_sums, 'dp', split_axis=0, concat_axis=0, tiled=True)  57.6 us
    all_to_all x1, starting transfers between devices, on_device(): lax.all_to_all(tile_sums, 'dp', split_axis=0, concat_axis=0, tiled=True)  23.5 us
    all_to_all x1, starting transfers between devices, on_device(): lax.all_to_all(outgoing, 'dp', split_axis=0, concat_axis=0, tiled=True)  7.45 us
    dot_general x2, matrix products, on_device(): jnp.einsum('scqm,mk->scqk', weights, label_matrix, preferred_element_type...  6.97 us
    dot_general x1, matrix products, on_device(): jnp.einsum('scqd,md->scqm', arrived, normalized, preferred_element_type=j...  6.75 us
  transfers between devices with their start and end apart: 3, of which 3 were waited for; matrix products, arithmetic and copies ran while one was open for 2% of the time, Pallas kernels for 0%

commit v1 on v0

v1 whole, which is shorter than its diff:
```python
import functools
import math

import jax
import jax.numpy as jnp
from jax import lax
from jax.experimental import pallas as pl
from jax.experimental.pallas import tpu as pltpu
from jax.sharding import PartitionSpec as P

ALPHA = 0.75
SOFTMAX_TEMPER = 0.05
EPSILON = 1e-06
GROUP = 8
SPLITS = 2
VMEM_BYTES = 60 * 1024 * 1024


def unitnorm_rows(features):
    wide = features.astype(jnp.float32)
    scale = lax.rsqrt(jnp.mean(wide * wide, axis=1, keepdims=True) + EPSILON)
    return (wide * scale / math.sqrt(wide.shape[1])).astype(jnp.bfloat16)


def weights_kernel(
    block_rows, tile_rows, step_tile, slot_block, slot_first, used, counts, memory, out, factor,
    held, total, sem
):
    step = pl.program_id(0)
    rows = memory.shape[0]

    @pl.when(step == 0)
    def _():
        copy = pltpu.make_async_copy(memory, held.at[pl.ds(0, rows)], sem)
        copy.start()
        copy.wait()

    @pl.when(step < used[0])
    def _():
        tile = step_tile[step]
        starts = [
            pl.multiple_of(slot_block[step * GROUP + j] * block_rows, block_rows)
            for j in range(GROUP)
        ]
        queries = jnp.concatenate([held[pl.ds(s, block_rows), :] for s in starts], axis=0)
        keys = held[pl.ds(pl.multiple_of(tile * tile_rows, tile_rows), tile_rows), :]
        scores = lax.dot_general(
            queries, keys, (((1,), (1,)), ((), ())), preferred_element_type=jnp.float32
        )
        columns = lax.broadcasted_iota(jnp.int32, scores.shape, 1)
        weights = jnp.where(
            columns < counts[tile], jnp.exp(scores * (1.0 / SOFTMAX_TEMPER)), 0.0
        ).astype(jnp.bfloat16)
        out[...] = weights
        sums = jnp.sum(weights.astype(jnp.float32), axis=1, keepdims=True)
        sums = jnp.broadcast_to(sums, (sums.shape[0], 128))
        for j in range(GROUP):
            where = pl.ds(starts[j], block_rows)
            old = jnp.where(slot_first[step * GROUP + j] == 1, 0.0, total[where, :])
            total[where, :] = old + sums[j * block_rows : (j + 1) * block_rows]

    @pl.when(step == pl.num_programs(0) - 1)
    def _():
        factor[...] = ALPHA / total[pl.ds(0, rows), :]


def labels_kernel(
    chunks, block_rows, own_slots, step_tile, slot_block, slot_first, used, own_block, own_first,
    me, weights, own_weights, prior, factor, own_prior, own_factor, out, total, own_total
):
    step = pl.program_id(0)
    tile_rows = prior.shape[0]

    def add(into, part, blocks, firsts, base, number):
        part = part.astype(jnp.bfloat16).astype(jnp.float32)
        for j in range(number):
            start = pl.multiple_of(blocks[base + j] * block_rows, block_rows)
            where = pl.ds(start, block_rows)
            old = jnp.where(firsts[base + j] == 1, 0.0, into[where, :])
            into[where, :] = old + part[j * block_rows : (j + 1) * block_rows]

    @pl.when(step < used[0])
    def _():
        part = jnp.dot(weights[...], prior[...], preferred_element_type=jnp.float32)
        add(total, part, slot_block, slot_first, step * GROUP, GROUP)

    @pl.when(step >= chunks)
    def _():
        tile = step - chunks
        rows = pl.ds(pl.multiple_of(tile * tile_rows, tile_rows), tile_rows)
        labels = total[rows, :] * factor[:, :1] + (1.0 - ALPHA) * prior[...].astype(jnp.float32)
        part = jnp.dot(
            own_weights[...], labels.astype(jnp.bfloat16), preferred_element_type=jnp.float32
        )
        add(own_total, part, own_block, own_first, tile * own_slots, own_slots)

    @pl.when(step == pl.num_programs(0) - 1)
    def _():
        spread = own_total[pl.ds(0, tile_rows), :] * own_factor[:, :1]
        out[...] = jnp.log(spread + (1.0 - ALPHA) * own_prior[...].astype(jnp.float32))


def on_device(features, class_bias, logits, tile_lists, valid_counts):
    devices = lax.axis_size("dp")
    twins = lax.axis_size("tensor")
    own_rows, width = features.shape
    block_count, listed = tile_lists.shape
    block_rows = own_rows // block_count
    rows = own_rows * devices
    blocks = block_count * devices
    requests = blocks * listed
    chunks = (requests + devices * (GROUP - 1)) // GROUP
    slots = chunks * GROUP
    me = lax.axis_index("dp").astype(jnp.int32)
    twin = lax.axis_index("tensor")

    normalized = unitnorm_rows(features)
    share = own_rows // twins
    mine = lax.dynamic_slice_in_dim(normalized, twin * share, share, 0)
    memory = lax.all_gather(mine, ("dp", "tensor"), axis=0, tiled=True)

    adjusted = logits.astype(jnp.float32) + class_bias[None, :]
    exponentials = jnp.exp(adjusted)
    row_totals = lax.psum(jnp.sum(exponentials, axis=1), "tensor")
    prior = (exponentials / row_totals[:, None]).astype(jnp.bfloat16)
    part_width = prior.shape[1] // SPLITS
    own_priors = [prior[:, s * part_width : (s + 1) * part_width] for s in range(SPLITS)]
    priors = [lax.all_gather(p, "dp", axis=0, tiled=True) for p in own_priors]

    small = jnp.concatenate([tile_lists.reshape(-1), valid_counts])
    small = lax.all_gather(small, "dp", axis=0, tiled=False)
    counts = small[:, -1]
    owners = small[:, :-1].reshape(-1)
    pairs = owners.reshape(-1, listed)
    firsts = jnp.stack([pairs[:, 0] < pairs[:, 1], pairs[:, 1] < pairs[:, 0]], axis=1)
    firsts = firsts.reshape(-1).astype(jnp.int32)
    hits = (owners[:, None] == jnp.arange(devices, dtype=jnp.int32)[None, :]).astype(jnp.int32)
    running = jnp.cumsum(hits, axis=0)
    earlier = jnp.sum((running - hits) * hits, axis=1)
    tile_chunks = (running[-1] + GROUP - 1) // GROUP
    ends = jnp.cumsum(tile_chunks)
    bases = ends - tile_chunks
    position = jnp.sum(hits * bases[None, :], axis=1) * GROUP + earlier
    matches = position[None, :] == jnp.arange(slots, dtype=jnp.int32)[:, None]
    request_ids = jnp.arange(requests, dtype=jnp.int32)
    filled = jnp.any(matches, axis=1)
    source = jnp.sum(jnp.where(matches, request_ids[None, :], 0), axis=1)
    slot_block = jnp.where(filled, source // listed, blocks)
    slot_first = jnp.sum(jnp.where(matches, firsts[None, :], 0), axis=1)
    used = ends[-1:]
    steps = jnp.minimum(jnp.arange(chunks, dtype=jnp.int32), used[0] - 1)
    chunk_tile = jnp.sum((steps[:, None] >= ends[None, :]).astype(jnp.int32), axis=1)
    step_tile = jnp.concatenate([chunk_tile, jnp.arange(devices, dtype=jnp.int32)])

    capacity = max(2, 64 // devices)
    own_requests = block_count * listed
    own_owners = tile_lists.reshape(-1)
    own_hits = (own_owners[:, None] == jnp.arange(devices, dtype=jnp.int32)[None, :]).astype(
        jnp.int32
    )
    own_earlier = jnp.sum((jnp.cumsum(own_hits, axis=0) - own_hits) * own_hits, axis=1)
    own_place = own_owners * capacity + own_earlier
    own_matches = (
        own_place[None, :] == jnp.arange(devices * capacity, dtype=jnp.int32)[:, None]
    )
    own_filled = jnp.any(own_matches, axis=1)

    def placed(values):
        return jnp.sum(jnp.where(own_matches, values[None, :], 0), axis=1)

    own_first = placed(lax.dynamic_slice_in_dim(firsts, me * own_requests, own_requests))
    own_slot = placed(lax.dynamic_slice_in_dim(position, me * own_requests, own_requests))
    own_block = jnp.where(
        own_filled, placed(jnp.arange(own_requests, dtype=jnp.int32) // listed), block_count
    )

    def one_chunk(step, tiles, sb, sf, n, *rest):
        return (jnp.minimum(step, n[0] - 1), 0)

    weights, factor = pl.pallas_call(
        functools.partial(weights_kernel, block_rows, own_rows),
        grid_spec=pltpu.PrefetchScalarGridSpec(
            num_scalar_prefetch=5,
            grid=(chunks,),
            in_specs=[pl.BlockSpec(memory_space=pl.ANY)],
            out_specs=[
                pl.BlockSpec((GROUP * block_rows, own_rows), one_chunk),
                pl.BlockSpec((rows, 128), lambda *a: (0, 0), pipeline_mode=pl.Buffered(1)),
            ],
            scratch_shapes=[
                pltpu.VMEM((rows + block_rows, width), jnp.bfloat16),
                pltpu.VMEM((rows + block_rows, 128), jnp.float32),
                pltpu.SemaphoreType.DMA,
            ],
        ),
        out_shape=[
            jax.ShapeDtypeStruct((slots * block_rows, own_rows), jnp.bfloat16),
            jax.ShapeDtypeStruct((rows, 128), jnp.float32),
        ],
        compiler_params=pltpu.CompilerParams(vmem_limit_bytes=VMEM_BYTES),
        cost_estimate=pl.CostEstimate(
            flops=2 * requests * block_rows * own_rows * width,
            bytes_accessed=rows * width * 2 + slots * block_rows * own_rows * 2,
            transcendentals=requests * block_rows * own_rows,
        ),
        name="weights",
    )(step_tile, slot_block, slot_first, used, counts, memory)

    own_weights = weights.reshape(slots, block_rows, own_rows)[own_slot]
    own_weights = own_weights.reshape(devices * capacity * block_rows, own_rows)
    own_factor = lax.dynamic_slice_in_dim(factor, me * own_rows, own_rows, 0)

    def tile_of(step, tiles, *rest):
        return (tiles[step], 0)

    def late_tile(step, *rest):
        return (jnp.maximum(step - chunks, 0), 0)

    def same(*a):
        return (0, 0)

    outs = []
    for piece, own_piece in zip(priors, own_priors):
        outs.append(
            pl.pallas_call(
                functools.partial(labels_kernel, chunks, block_rows, capacity),
                grid_spec=pltpu.PrefetchScalarGridSpec(
                    num_scalar_prefetch=7,
                    grid=(chunks + devices,),
                    in_specs=[
                        pl.BlockSpec((GROUP * block_rows, own_rows), one_chunk),
                        pl.BlockSpec((capacity * block_rows, own_rows), late_tile),
                        pl.BlockSpec((own_rows, part_width), tile_of),
                        pl.BlockSpec((own_rows, 128), late_tile),
                        pl.BlockSpec((own_rows, part_width), same),
                        pl.BlockSpec((own_rows, 128), same),
                    ],
                    out_specs=pl.BlockSpec((own_rows, part_width), same),
                    scratch_shapes=[
                        pltpu.VMEM((rows + block_rows, part_width), jnp.float32),
                        pltpu.VMEM((own_rows + block_rows, part_width), jnp.float32),
                    ],
                ),
                out_shape=jax.ShapeDtypeStruct((own_rows, part_width), jnp.float32),
                compiler_params=pltpu.CompilerParams(vmem_limit_bytes=VMEM_BYTES),
                cost_estimate=pl.CostEstimate(
                    flops=2 * requests * block_rows * own_rows * part_width,
                    bytes_accessed=slots * block_rows * own_rows * 2,
                    transcendentals=0,
                ),
                name="labels",
            )(
                step_tile, slot_block, slot_first, used, own_block, own_first, me.reshape(1),
                weights, own_weights, piece, factor, own_piece, own_factor,
            )
        )
    return jnp.concatenate(outs, axis=1)


def solution(mesh):
    in_specs = (P("dp", None), P("tensor"), P("dp", "tensor"), P("dp", None), P("dp"))
    out_specs = P("dp", "tensor")
    return jax.shard_map(
        on_device, mesh=mesh, in_specs=in_specs, out_specs=out_specs, check_vma=False
    )
```

time: 318 us -> 350 us (1.10); the launches traced: 318 us -> 345 us
  Pallas kernels: 0 us -> 178 us
  blocking collectives: 89.2 us -> 17.3 us
  waiting for transfers between devices: 149 us -> 107 us
  starting transfers between devices: 36.6 us -> 0.09 us
  between operations: 0.83 us -> 15.2 us
  matrix products: 13.7 us -> 0 us
    pallas_call x0 -> x3, Pallas kernels: none -> 178 us  [the longest x2 121 us: on_device(): pl.pallas_call(functools.partial(labels_kernel, chunks, block_rows, capac...]
    all_to_all x3 -> x0, waiting for transfers between devices: 149 us -> none  [the longest x1 91.1 us: on_device(): lax.all_to_all(outgoing, 'dp', split_axis=0, concat_axis=0, tiled=True)]
    all_gather x0 -> x3, waiting for transfers between devices: none -> 106 us  [the longest x1 106 us: on_device(): memory = lax.all_gather(mine, ('dp', 'tensor'), axis=0, tiled=True)]
    all_to_all x1 -> x0, blocking collectives: 85 us -> none  [on_device(): lax.all_to_all(partial_sums, 'dp', split_axis=0, concat_axis=0, tiled=True)]
    all_to_all x3 -> x0, starting transfers between devices: 36.6 us -> none  [the longest x1 23.5 us: on_device(): lax.all_to_all(tile_sums, 'dp', split_axis=0, concat_axis=0, tiled=True)]
    dot_general x3 -> x0, matrix products: 13.7 us -> none  [the longest x2 6.97 us: on_device(): jnp.einsum('scqm,mk->scqk', weights, label_matrix, preferred_element_type...]
    unnamed x0 -> x1, blocking collectives: none -> 12.9 us
    select_n x3 -> x5, other arithmetic: 5.26 us -> 1.16 us  [the longest x1 0.6 us: on_device(): slot_block = jnp.where(filled, source // listed, blocks)]
  transfers between devices with their start and end apart: 3 -> 3, of which waited for: 3 -> 1; matrix products, arithmetic and copies ran while one was open for 2% -> 6% of each run, Pallas kernels for 0% -> 34%
where the time goes in v1:
time: 350 us; the launch traced here: 345 us
  Pallas kernels  178 us (51%)
  waiting for transfers between devices  107 us (31%)
  blocking collectives  17.3 us (5%)
  local copies, waits for them, and re-layouts  15.2 us (4%)
  between operations  15.2 us (4%)
  other arithmetic  12.4 us (4%)
    pallas_call x2, Pallas kernels, on_device(): pl.pallas_call(functools.partial(labels_kernel, chunks, block_rows, capac...  121 us
    all_gather x1, waiting for transfers between devices, on_device(): memory = lax.all_gather(mine, ('dp', 'tensor'), axis=0, tiled=True)  106 us
    pallas_call x1, Pallas kernels, on_device(): pl.pallas_call(functools.partial(weights_kernel, block_rows, own_rows), g...  56.9 us
    unnamed x1, blocking collectives  12.9 us
    gather x1, local copies, waits for them, and re-layouts, on_device(): own_weights = weights.reshape(slots, block_rows, own_rows)[own_slot]  9.03 us
  transfers between devices with their start and end apart: 3, of which 1 were waited for; matrix products, arithmetic and copies ran while one was open for 6% of the time, Pallas kernels for 34%

profile of v1, /device:TPU:1, one launch (start us, length us, event | category | flops | bytes accessed | tf_op | source)
XLA Modules:
  0.0 345.1 jit_solution(17450714019780032258)
XLA Ops:
  6.5 1.6 convert_element_type.41
  8.1 0.1 copy-done
  8.2 0.3 multiply_reduce_fusion
  8.6 0.1 dynamic-slice.1
  8.7 1.0 fusion.2
  9.8 0.3 fusion
  10.1 4.4 %psum.7 = f32[512]{0:T(512)S(1)} all-reduce(f32[512]{0:T(512)S(1)} %fusion), channel_id=1, replica_groups=mesh['dp'=16,'tensor'=2] {'tensor'}, use_global_device_ids=true, to_apply=%region_17.18 | all-reduce | flops 512 | bytes 4096 | tf_op jit(solution)/shard_map/psum | solution.py:124
  14.5 0.3 divide_convert_fusion
  14.9 1.0 fusion.16
  15.9 0.7 all-gather.7.cloned.1.call-update
  17.3 0.1 copy.23
  17.4 0.1 reshape.164
  17.5 0.6 dynamic-slice
  18.7 0.2 add_dynamic-update-slice_fusion
  18.9 12.9 %all-reduce = s32[528]{0:T(1024)S(1)} all-reduce(s32[528]{0:T(1024)S(1)} %add_dynamic-update-slice_fusion), channel_id=2, replica_groups=mesh['dp'=16,'tensor'=2] {'dp'}, use_global_device_ids=true, to_apply=%add | all-reduce | flops 528 | bytes 4224
  31.8 0.1 reshape.179
  32.0 1.1 reduce-window.10
  33.1 0.2 slice_reduce_fusion
  33.4 0.2 fusion.11
  33.6 0.1 copy.25
  33.8 0.5 slice.51
  34.3 0.1 reduce.2
  34.5 0.1 reshape_reshape.3
  34.6 0.1 slice_compare_fusion.1
  34.7 0.1 copy.28
  34.8 0.1 copy.27
  34.9 0.1 copy.29
  35.0 0.1 reshape.170
  35.3 0.2 fusion.9
  35.5 0.1 select_reduce_fusion.3
  35.6 0.1 dynamic_slice.14
  36.4 0.1 convert_reduce_fusion
  36.5 0.7 pad_add_fusion.step_tile
  37.1 0.2 select_reduce_fusion.7
  37.3 0.7 select_reduce_fusion.4
  38.0 0.8 slice_reduce_fusion.1.counts
  38.8 0.1 fusion.5
  38.9 0.2 fusion.3
  39.1 1.0 select_reduce_fusion
  40.1 0.5 broadcast_select_fusion.own_block
  40.6 0.6 fusion.13.slot_block
  41.2 106.3 %all-gather.5.cloned.1.call-done.memory = bf16[8192,1280]{1,0:T(8,128)(2,1)} async-done(((bf16[256,1280]{1,0:T(8,128)(2,1)}), bf16[8192,1280]{1,0:T(8,128)(2,1)}) %all-gather.5.cloned.1.call-update) | async-done | bytes 20971536 | tf_op jit(solution)/shard_map/all_gather | solution.py:120
  147.5 56.9 %weights.1 = (bf16[19968,512]{1,0:T(8,128)(2,1)}, f32[8192,128]{1,0:T(8,128)}) custom-call(s32[94]{0:T(128)} %pad_add_fusion.step_tile, s32[624]{0:T(1024)} %fusion.13.slot_block, s32[624]{0:T(1024)} %get-tuple-element.9.slot_first, s32[1]{0:T(128)} %bitcast.4.used, s32[16]{0:T(128)} %slice_reduce_fusion.1.counts, ...), custom_call_target="tpu_custom_call" | custom-call | flops 21474836480 | bytes 41418752 | tf_op jit(solution)/shard_map/weights/pallas_call | solution.py:180
  204.4 9.0 %gather_fusion = bf16[64,32,512]{2,1,0:T(8,128)(2,1)} fusion(bf16[624,32,512]{2,1,0:T(8,128)(2,1)} %bitcast.33, s32[1024]{0:T(1024)S(1)} %pad_clamp_fusion), kind=kCustom, calls=%fused_computation | custom fusion | bytes 4194560 | tf_op jit(solution)/shard_map/gather | solution.py:209
  213.4 1.7 constant_dynamic-slice_fusion.own_factor
  215.1 60.7 %labels.3 = f32[512,384]{1,0:T(8,128)} custom-call(s32[94]{0:T(128)} %pad_add_fusion.step_tile, s32[624]{0:T(1024)} %fusion.13.slot_block, s32[624]{0:T(1024)} %get-tuple-element.9.slot_first, s32[1]{0:T(128)} %bitcast.4.used, s32[64]{0:T(128)} %broadcast_select_fusion.own_block, s32[64]{0:T(128)} %get-tuple-element.14.own_first, s32[1]{0:T(128)} %bitcast.5.me, ...), custom_call_target="tpu_custom_call" | custom-call | flops 6442450944 | bytes 20447232 | tf_op jit(solution)/shard_map/labels/pallas_call | solution.py:225
  275.8 60.4 %labels.2 = f32[512,384]{1,0:T(8,128)} custom-call(s32[94]{0:T(128)} %pad_add_fusion.step_tile, s32[624]{0:T(1024)} %fusion.13.slot_block, s32[624]{0:T(1024)} %get-tuple-element.9.slot_first, s32[1]{0:T(128)} %bitcast.4.used, s32[64]{0:T(128)} %broadcast_select_fusion.own_block, s32[64]{0:T(128)} %get-tuple-element.14.own_first, s32[1]{0:T(128)} %bitcast.5.me, ...), custom_call_target="tpu_custom_call" | custom-call | flops 6442450944 | bytes 20447232 | tf_op jit(solution)/shard_map/labels/pallas_call | solution.py:225
  336.2 2.4 pad_maximum_fusion
  (39 shorter events, 0.7 us)
Async XLA Ops:
  6.5 140.9 %all-gather.5.cloned.1.call-start = ((), (), s32[]{:S(2)}) async-start(), calls=%async_computation | async-start | bytes 21626880 | tf_op jit(solution)/shard_map/all_gather | solution.py:120
  6.5 1.7 copy-start
  8.6 1.2 copy-start.1
  8.6 1.2 copy-start.3
  9.7 205.4 %all-gather.9.cloned.1.call-start = ((), (), s32[]{:S(2)}) async-start(), calls=%async_computation.2 | async-start | bytes 6684672 | tf_op jit(solution)/shard_map/all_gather | solution.py:128
  14.8 2.5 copy-start.4
  14.8 2.6 copy-start.5
  15.9 259.9 %all-gather.7.cloned.1.call-start = ((), (), s32[]{:S(2)}) async-start(), calls=%async_computation.1 | async-start | bytes 6684672 | tf_op jit(solution)/shard_map/all_gather | solution.py:128
  275.8 60.4 %copy-start.2 = (f32[512,384]{1,0:T(8,128)S(1)}, f32[512,384]{1,0:T(8,128)}, u32[]{:S(2)}) copy-start(f32[512,384]{1,0:T(8,128)} %labels.3) | copy-start | bytes 2359300
Sparse Core Ops, SparseCore 0:
  10.2 137.2 all-gather.4
  149.7 60.7 all-gather.8
  212.8 59.9 all-gather.6

commit v2 on v1

--- a/solution.py
+++ b/solution.py
@@ -11,8 +11,7 @@
 ALPHA = 0.75
 SOFTMAX_TEMPER = 0.05
 EPSILON = 1e-06
-GROUP = 8
-SPLITS = 2
+GROUP = 16
 VMEM_BYTES = 60 * 1024 * 1024
 
 
@@ -98,6 +97,177 @@
     def _():
         spread = own_total[pl.ds(0, tile_rows), :] * own_factor[:, :1]
         out[...] = jnp.log(spread + (1.0 - ALPHA) * own_prior[...].astype(jnp.float32))
+
+
+def gather_kernel(features, labels, memory, priors, recv, send, local):
+    dp, y = lax.axis_index("dp"), lax.axis_index("tensor")
+    z, x, c = dp // 4, (dp // 2) % 2, dp % 2
+    rows = features.shape[0]
+    half = rows // 2
+
+    def index(zz, xx):
+        return zz * 4 + xx * 2 + c
+
+    def region(t, kind):
+        if kind == 2:
+            return priors.at[pl.ds(pl.multiple_of(t * rows, rows), rows)]
+        h = y if kind == 0 else 1 - y
+        return memory.at[pl.ds(pl.multiple_of(t * rows + h * half, half), half)]
+
+    def own_region(kind):
+        if kind == 2:
+            return labels
+        h = y if kind == 0 else 1 - y
+        return features.at[pl.ds(pl.multiple_of(h * half, half), half)]
+
+    def partner(way):
+        if way == 0:
+            return {"dp": dp - 4}
+        if way == 1:
+            return {"dp": dp + 4}
+        if way == 2:
+            return {"dp": dp + 2 - 4 * x}
+        if way == 3:
+            return {"tensor": 1 - y}
+        return {"dp": dp + 1 - 2 * c}
+
+    def reach(way):
+        if way == 0:
+            return z > 0
+        if way == 1:
+            return z < 3
+        return None
+
+    def guarded(conditions, body):
+        conditions = [q for q in conditions if q is not None]
+        if not conditions:
+            body()
+        else:
+            both = conditions[0]
+            for q in conditions[1:]:
+                both = jnp.logical_and(both, q)
+            pl.when(both)(body)
+
+    sent = []
+
+    def copy(zz, xx, kind, way, own):
+        t = index(zz, xx)
+        arrives = 1 if way == 3 else kind
+        return pltpu.make_async_remote_copy(
+            src_ref=own_region(kind) if own else region(t, kind),
+            dst_ref=region(t, kind),
+            send_sem=send.at[zz * 2 + xx, kind, way],
+            recv_sem=recv.at[t, arrives],
+            device_id=partner(way),
+            device_id_type=pl.DeviceIdType.MESH,
+        )
+
+    def push(zz, xx, kind, ways, exists=None, own=False):
+        for way in ways:
+            guards = (exists, reach(way))
+            guarded(guards, lambda way=way: copy(zz, xx, kind, way, own).start())
+            sent.append((guards, zz, xx, kind, way, own))
+
+    def landed(t, kind):
+        pltpu.make_async_remote_copy(
+            src_ref=region(t, kind), dst_ref=region(t, kind),
+            send_sem=send.at[0, 0, 0], recv_sem=recv.at[t, kind],
+            device_id=partner(4), device_id_type=pl.DeviceIdType.MESH,
+        ).wait_recv()
+
+    def column(distance):
+        if distance == 0:
+            return [(z, None, (0, 1))]
+        return [
+            (z - distance, z >= distance, (1,)),
+            (z + distance, z + distance < 4, (0,)),
+        ]
+
+    def near(distance, kind):
+        for zz, exists, ways in column(distance):
+            guarded((exists,), lambda zz=zz: landed(index(zz, x), kind))
+            onward = ways + ((2, 3, 4) if kind == 0 else (2, 4))
+            push(zz, x, kind, onward, exists)
+
+    def across(distance, kind):
+        for zz, exists, _ in column(distance):
+            guarded((exists,), lambda zz=zz: landed(index(zz, 1 - x), kind))
+            push(zz, 1 - x, kind, (3, 4) if kind == 0 else (4,), exists)
+
+    def mirrored(distance, xx):
+        for zz, exists, _ in column(distance):
+            guarded((exists,), lambda zz=zz: landed(index(zz, xx), 1))
+            push(zz, xx, 1, (4,), exists)
+
+    barrier = pltpu.get_barrier_semaphore()
+    for way in range(5):
+        guarded(
+            (reach(way),),
+            lambda way=way: pl.semaphore_signal(
+                barrier, inc=1, device_id=partner(way), device_id_type=pl.DeviceIdType.MESH
+            ),
+        )
+    pl.semaphore_wait(barrier, 4 + z * (3 - z) // 2)
+
+    push(z, x, 0, (0, 1, 2, 4), own=True)
+    keep = pl.ds(pl.multiple_of(dp * rows, rows), rows)
+    copies = [
+        pltpu.make_async_copy(features, memory.at[keep], local.at[0]),
+        pltpu.make_async_copy(labels, priors.at[keep], local.at[1]),
+    ]
+    for one in copies:
+        one.start()
+    for distance in (1, 2, 3):
+        near(distance, 0)
+        across(distance - 1, 0)
+        if distance == 2:
+            push(z, x, 2, (0, 1, 2, 4), own=True)
+            push(z, x, 1, (4,), own=True)
+    across(3, 0)
+    for distance in (1, 2, 3):
+        near(distance, 2)
+        across(distance - 1, 2)
+        mirrored(distance, x)
+        mirrored(distance - 1, 1 - x)
+    mirrored(3, 1 - x)
+    across(3, 2)
+    for zz in range(4):
+        for xx in range(2):
+            for kind in range(3):
+                landed(zz * 4 + xx * 2 + 1 - c, kind)
+    for guards, zz, xx, kind, way, own in sent:
+        guarded(
+            guards,
+            lambda zz=zz, xx=xx, kind=kind, way=way, own=own: copy(
+                zz, xx, kind, way, own
+            ).wait_send(),
+        )
+    for one in copies:
+        one.wait()
+
+
+def gather_all(normalized, prior, devices):
+    rows, width = normalized.shape
+    classes = prior.shape[1]
+    return pl.pallas_call(
+        gather_kernel,
+        in_specs=[pl.BlockSpec(memory_space=pl.ANY)] * 2,
+        out_specs=[pl.BlockSpec(memory_space=pl.ANY)] * 2,
+        out_shape=[
+            jax.ShapeDtypeStruct((devices * rows, width), normalized.dtype),
+            jax.ShapeDtypeStruct((devices * rows, classes), prior.dtype),
+        ],
+        scratch_shapes=[
+            pltpu.SemaphoreType.DMA((devices, 3)),
+            pltpu.SemaphoreType.DMA((8, 3, 5)),
+            pltpu.SemaphoreType.DMA((2,)),
+        ],
+        compiler_params=pltpu.CompilerParams(collective_id=0, has_side_effects=True),
+        cost_estimate=pl.CostEstimate(
+            flops=0, bytes_accessed=2 * devices * rows * (width + classes) * 2, transcendentals=0
+        ),
+        name="gather",
+    )(normalized, prior)
 
 
 def on_device(features, class_bias, logits, tile_lists, valid_counts):
@@ -115,17 +285,22 @@
     twin = lax.axis_index("tensor")
 
     normalized = unitnorm_rows(features)
-    share = own_rows // twins
-    mine = lax.dynamic_slice_in_dim(normalized, twin * share, share, 0)
-    memory = lax.all_gather(mine, ("dp", "tensor"), axis=0, tiled=True)
-
     adjusted = logits.astype(jnp.float32) + class_bias[None, :]
     exponentials = jnp.exp(adjusted)
     row_totals = lax.psum(jnp.sum(exponentials, axis=1), "tensor")
     prior = (exponentials / row_totals[:, None]).astype(jnp.bfloat16)
-    part_width = prior.shape[1] // SPLITS
-    own_priors = [prior[:, s * part_width : (s + 1) * part_width] for s in range(SPLITS)]
-    priors = [lax.all_gather(p, "dp", axis=0, tiled=True) for p in own_priors]
+    grid_links = devices == 16 and twins == 2
+    splits = 1 if grid_links else 2
+    part_width = prior.shape[1] // splits
+    own_priors = [prior[:, s * part_width : (s + 1) * part_width] for s in range(splits)]
+    if grid_links:
+        memory, gathered = gather_all(normalized, prior, devices)
+        priors = [gathered]
+    else:
+        share = own_rows // twins
+        mine = lax.dynamic_slice_in_dim(normalized, twin * share, share, 0)
+        memory = lax.all_gather(mine, ("dp", "tensor"), axis=0, tiled=True)
+        priors = [lax.all_gather(p, "dp", axis=0, tiled=True) for p in own_priors]
 
     small = jnp.concatenate([tile_lists.reshape(-1), valid_counts])
     small = lax.all_gather(small, "dp", axis=0, tiled=False)
@@ -254,7 +429,7 @@
                 weights, own_weights, piece, factor, own_piece, own_factor,
             )
         )
-    return jnp.concatenate(outs, axis=1)
+    return outs[0] if splits == 1 else jnp.concatenate(outs, axis=1)
 
 
 def solution(mesh):

time: 350 us -> 284 us (0.81)
  waiting for transfers between devices: 107 us -> 0 us
  Pallas kernels: 178 us -> 237 us
  between operations: 15.2 us -> 2.08 us
    pallas_call x0 -> x1, Pallas kernels: none -> 134 us  [gather_all(): pl.pallas_call(gather_kernel, in_specs=[pl.BlockSpec(memory_space=pl.ANY)...]
    all_gather x3 -> x0, waiting for transfers between devices: 106 us -> none  [the longest x1 106 us: on_device(): memory = lax.all_gather(mine, ('dp', 'tensor'), axis=0, tiled=True)]
    pallas_call x2 -> x1, Pallas kernels: 121 us -> 53.3 us  [on_device(): pl.pallas_call(functools.partial(labels_kernel, chunks, block_rows, capac...]
    pallas_call x1, Pallas kernels: 56.9 us -> 48.8 us  [on_device(): pl.pallas_call(functools.partial(weights_kernel, block_rows, own_rows), g...]
  transfers between devices with their start and end apart: 3 -> 0, of which waited for: 1 -> 0; matrix products, arithmetic and copies ran while one was open for 6% -> 0% of each run, Pallas kernels for 34% -> 0%
where the time goes in v2:
time: 284 us; the launch traced here: 279 us
  Pallas kernels  237 us (83%)
  local copies, waits for them, and re-layouts  16.5 us (6%)
  blocking collectives  14.5 us (5%)
  other arithmetic  9.55 us (3%)
    pallas_call x1, Pallas kernels, gather_all(): pl.pallas_call(gather_kernel, in_specs=[pl.BlockSpec(memory_space=pl.ANY)...  134 us
    pallas_call x1, Pallas kernels, on_device(): pl.pallas_call(functools.partial(labels_kernel, chunks, block_rows, capac...  53.3 us
    pallas_call x1, Pallas kernels, on_device(): pl.pallas_call(functools.partial(weights_kernel, block_rows, own_rows), g...  48.8 us
    unnamed x1, blocking collectives  10.7 us
    gather x1, local copies, waits for them, and re-layouts, on_device(): own_weights = weights.reshape(slots, block_rows, own_rows)[own_slot]  10.1 us

profile of v2, /device:TPU:1, one launch (start us, length us, event | category | flops | bytes accessed | tf_op | source)
XLA Modules:
  0.0 279.1 jit_solution(3967523231781647317)
XLA Ops:
  0.0 1.3 dynamic-slice
  2.6 0.8 copy.23
  3.4 0.1 reshape.163
  3.5 0.2 add_dynamic-update-slice_fusion
  3.7 10.7 %all-reduce = s32[528]{0:T(1024)S(1)} all-reduce(s32[528]{0:T(1024)S(1)} %add_dynamic-update-slice_fusion), channel_id=2, replica_groups=mesh['dp'=16,'tensor'=2] {'dp'}, use_global_device_ids=true, to_apply=%add | all-reduce | flops 528 | bytes 4224
  14.4 0.1 reshape.178
  14.5 0.1 eq.64
  14.5 1.1 reduce-window.10
  15.7 0.2 slice_reduce_fusion
  15.9 0.1 bitcast_bitcast_fusion
  16.0 0.2 fusion.12
  16.2 0.1 copy.25
  16.4 0.6 slice.43
  17.5 0.1 reduce.2
  17.7 0.1 convert_reduce_fusion
  17.7 0.6 pad_add_fusion.step_tile
  18.4 0.2 fusion.10
  18.5 0.1 eq.68
  18.6 0.1 select_reduce_fusion.3
  18.7 0.2 fusion.4
  19.0 0.1 reshape_reshape.3
  19.1 0.1 slice_compare_fusion.1
  19.2 0.1 copy.28
  19.3 0.1 copy.27
  19.4 0.1 copy.29
  19.6 0.1 reshape.169
  19.7 1.0 select_reduce_fusion
  20.7 0.6 fusion.14.slot_block
  21.3 0.1 fusion.7
  21.3 0.1 reduce_window_sum.35
  21.4 0.2 select_reduce_fusion.7
  21.6 0.1 fusion.6
  21.7 0.1 dynamic_slice.10
  21.8 0.1 dynamic_slice.9
  21.8 0.6 select_reduce_fusion.4
  22.5 0.5 broadcast_select_fusion.own_block
  23.0 0.7 slice_reduce_fusion.1.counts
  23.7 0.3 fusion
  24.0 0.0 copy-start.2
  24.1 1.4 fusion.2.features
  25.5 0.3 fusion.3
  25.8 3.8 %psum.7 = f32[512]{0:T(512)S(1)} all-reduce(f32[512]{0:T(512)S(1)} %fusion.3), channel_id=1, replica_groups=mesh['dp'=16,'tensor'=2] {'tensor'}, use_global_device_ids=true, to_apply=%region_16.17 | all-reduce | flops 512 | bytes 4096 | tf_op jit(solution)/shard_map/psum | solution.py:290
  29.6 1.2 divide_convert_fusion.labels.own_prior
  30.8 134.5 %gather.7 = (bf16[8192,1280]{1,0:T(8,128)(2,1)}, bf16[8192,768]{1,0:T(8,128)(2,1)}) custom-call(bf16[512,1280]{1,0:T(8,128)(2,1)} %fusion.2.features, bf16[512,768]{1,0:T(8,128)(2,1)} %divide_convert_fusion.labels.own_prior), custom_call_target="tpu_custom_call" | custom-call | bytes 67108864 | tf_op jit(solution)/shard_map/gather/pallas_call | solution.py:252
  165.3 48.8 %weights.1 = (bf16[24064,512]{1,0:T(8,128)(2,1)}, f32[8192,128]{1,0:T(8,128)}) custom-call(s32[63]{0:T(128)} %pad_add_fusion.step_tile, s32[752]{0:T(1024)} %fusion.14.slot_block, s32[752]{0:T(1024)} %get-tuple-element.13.slot_first, s32[1]{0:T(128)} %bitcast.4.used, s32[16]{0:T(128)} %slice_reduce_fusion.1.counts, bf16[8192,1280]{1,0:T(8,128)(2,1)} %get-tuple-element.9.memory), custom_call_target="tpu_custom_call" | custom-call | flops 21474836480 | bytes 45613056 | tf_op jit(solution)/shard_map/weights/pallas_call | solution.py:355
  214.1 10.1 %gather_fusion = bf16[64,32,512]{2,1,0:T(8,128)(2,1)} fusion(bf16[752,32,512]{2,1,0:T(8,128)(2,1)} %bitcast.37, s32[1024]{0:T(1024)S(1)} %pad_clamp_fusion), kind=kCustom, calls=%fused_computation | custom fusion | bytes 4194560 | tf_op jit(solution)/shard_map/gather | solution.py:384
  224.2 1.7 constant_dynamic-slice_fusion.own_factor
  225.8 53.3 %labels.1 = f32[512,768]{1,0:T(8,128)} custom-call(s32[63]{0:T(128)} %pad_add_fusion.step_tile, s32[752]{0:T(1024)} %fusion.14.slot_block, s32[752]{0:T(1024)} %get-tuple-element.13.slot_first, s32[1]{0:T(128)} %bitcast.4.used, s32[64]{0:T(128)} %broadcast_select_fusion.own_block, s32[64]{0:T(128)} %get-tuple-element.18.own_first, s32[1]{0:T(128)} %bitcast.5.me, ...), custom_call_target="tpu_custom_call" | custom-call | flops 12884901888 | bytes 24641536 | tf_op jit(solution)/shard_map/labels/pallas_call | solution.py:400
  (20 shorter events, 0.2 us)
Async XLA Ops:
  0.0 23.7 %copy-start = (bf16[512,1280]{1,0:T(8,128)(2,1)S(1)}, bf16[512,1280]{1,0:T(8,128)(2,1)}, u32[]{:S(2)}) copy-start(bf16[512,1280]{1,0:T(8,128)(2,1)} %param.5) | copy-start | bytes 3932164
  24.0 1.5 copy-start.1
  24.0 1.5 copy-start.2

commit v3 on v2

--- a/solution.py
+++ b/solution.py
@@ -41,22 +41,26 @@
             pl.multiple_of(slot_block[step * GROUP + j] * block_rows, block_rows)
             for j in range(GROUP)
         ]
-        queries = jnp.concatenate([held[pl.ds(s, block_rows), :] for s in starts], axis=0)
         keys = held[pl.ds(pl.multiple_of(tile * tile_rows, tile_rows), tile_rows), :]
-        scores = lax.dot_general(
-            queries, keys, (((1,), (1,)), ((), ())), preferred_element_type=jnp.float32
-        )
-        columns = lax.broadcasted_iota(jnp.int32, scores.shape, 1)
-        weights = jnp.where(
-            columns < counts[tile], jnp.exp(scores * (1.0 / SOFTMAX_TEMPER)), 0.0
-        ).astype(jnp.bfloat16)
-        out[...] = weights
-        sums = jnp.sum(weights.astype(jnp.float32), axis=1, keepdims=True)
-        sums = jnp.broadcast_to(sums, (sums.shape[0], 128))
-        for j in range(GROUP):
-            where = pl.ds(starts[j], block_rows)
-            old = jnp.where(slot_first[step * GROUP + j] == 1, 0.0, total[where, :])
-            total[where, :] = old + sums[j * block_rows : (j + 1) * block_rows]
+        some = GROUP // 2
+        for begin in range(0, GROUP, some):
+            queries = jnp.concatenate(
+                [held[pl.ds(s, block_rows), :] for s in starts[begin : begin + some]], axis=0
+            )
+            scores = lax.dot_general(
+                queries, keys, (((1,), (1,)), ((), ())), preferred_element_type=jnp.float32
+            )
+            columns = lax.broadcasted_iota(jnp.int32, scores.shape, 1)
+            weights = jnp.where(
+                columns < counts[tile], jnp.exp(scores * (1.0 / SOFTMAX_TEMPER)), 0.0
+            ).astype(jnp.bfloat16)
+            out[begin * block_rows : (begin + some) * block_rows, :] = weights
+            sums = jnp.sum(weights.astype(jnp.float32), axis=1, keepdims=True)
+            sums = jnp.broadcast_to(sums, (sums.shape[0], 128))
+            for j in range(some):
+                where = pl.ds(starts[begin + j], block_rows)
+                old = jnp.where(slot_first[step * GROUP + begin + j] == 1, 0.0, total[where, :])
+                total[where, :] = old + sums[j * block_rows : (j + 1) * block_rows]
 
     @pl.when(step == pl.num_programs(0) - 1)
     def _():
@@ -65,41 +69,54 @@
 
 def labels_kernel(
     chunks, block_rows, own_slots, step_tile, slot_block, slot_first, used, own_block, own_first,
-    me, weights, own_weights, prior, factor, own_prior, own_factor, out, total, own_total
+    own_slot, me, weights, *rest
 ):
+    own_weights = rest[:own_slots]
+    prior, factor, own_prior, own_factor, out, total, own_total = rest[own_slots:]
     step = pl.program_id(0)
-    tile_rows = prior.shape[0]
-
-    def add(into, part, blocks, firsts, base, number):
-        part = part.astype(jnp.bfloat16).astype(jnp.float32)
+    tile_rows, width = prior.shape
+    piece = 256 if width % 256 == 0 else 128
+    pieces = [slice(p, p + piece) for p in range(0, width, piece)]
+
+    def add(into, part, cut, blocks, firsts, base, number):
         for j in range(number):
             start = pl.multiple_of(blocks[base + j] * block_rows, block_rows)
             where = pl.ds(start, block_rows)
-            old = jnp.where(firsts[base + j] == 1, 0.0, into[where, :])
-            into[where, :] = old + part[j * block_rows : (j + 1) * block_rows]
+            old = jnp.where(firsts[base + j] == 1, 0.0, into[where, cut])
+            into[where, cut] = old + part[j * block_rows : (j + 1) * block_rows]
+
+    def wide(lanes):
+        return jnp.concatenate([lanes] * (piece // 128), axis=1)
 
     @pl.when(step < used[0])
     def _():
-        part = jnp.dot(weights[...], prior[...], preferred_element_type=jnp.float32)
-        add(total, part, slot_block, slot_first, step * GROUP, GROUP)
+        for cut in pieces:
+            part = jnp.dot(weights[...], prior[:, cut], preferred_element_type=jnp.float32)
+            add(total, part, cut, slot_block, slot_first, step * GROUP, GROUP)
 
     @pl.when(step >= chunks)
     def _():
         tile = step - chunks
         rows = pl.ds(pl.multiple_of(tile * tile_rows, tile_rows), tile_rows)
-        labels = total[rows, :] * factor[:, :1] + (1.0 - ALPHA) * prior[...].astype(jnp.float32)
-        part = jnp.dot(
-            own_weights[...], labels.astype(jnp.bfloat16), preferred_element_type=jnp.float32
-        )
-        add(own_total, part, own_block, own_first, tile * own_slots, own_slots)
+        sent = jnp.concatenate([w[...] for w in own_weights], axis=0)
+        scale = wide(factor[...])
+        for cut in pieces:
+            labels = total[rows, cut] * scale + (1.0 - ALPHA) * prior[:, cut].astype(jnp.float32)
+            part = jnp.dot(
+                sent, labels.astype(jnp.bfloat16), preferred_element_type=jnp.float32
+            )
+            add(own_total, part, cut, own_block, own_first, tile * own_slots, own_slots)
 
     @pl.when(step == pl.num_programs(0) - 1)
     def _():
-        spread = own_total[pl.ds(0, tile_rows), :] * own_factor[:, :1]
-        out[...] = jnp.log(spread + (1.0 - ALPHA) * own_prior[...].astype(jnp.float32))
-
-
-def gather_kernel(features, labels, memory, priors, recv, send, local):
+        scale = wide(own_factor[...])
+        for cut in pieces:
+            spread = own_total[pl.ds(0, tile_rows), cut] * scale
+            spread += (1.0 - ALPHA) * own_prior[:, cut].astype(jnp.float32)
+            out[:, cut] = jnp.log(spread)
+
+
+def gather_kernel(features, lists, memory, all_lists, recv, send, local):
     dp, y = lax.axis_index("dp"), lax.axis_index("tensor")
     z, x, c = dp // 4, (dp // 2) % 2, dp % 2
     rows = features.shape[0]
@@ -110,13 +127,13 @@
 
     def region(t, kind):
         if kind == 2:
-            return priors.at[pl.ds(pl.multiple_of(t * rows, rows), rows)]
+            return all_lists.at[t]
         h = y if kind == 0 else 1 - y
         return memory.at[pl.ds(pl.multiple_of(t * rows + h * half, half), half)]
 
     def own_region(kind):
         if kind == 2:
-            return labels
+            return lists
         h = y if kind == 0 else 1 - y
         return features.at[pl.ds(pl.multiple_of(h * half, half), half)]
 
@@ -210,27 +227,28 @@
     pl.semaphore_wait(barrier, 4 + z * (3 - z) // 2)
 
     push(z, x, 0, (0, 1, 2, 4), own=True)
+    push(z, x, 2, (0, 1, 2, 4), own=True)
+    push(z, x, 1, (4,), own=True)
     keep = pl.ds(pl.multiple_of(dp * rows, rows), rows)
     copies = [
         pltpu.make_async_copy(features, memory.at[keep], local.at[0]),
-        pltpu.make_async_copy(labels, priors.at[keep], local.at[1]),
+        pltpu.make_async_copy(lists, all_lists.at[dp], local.at[1]),
     ]
     for one in copies:
         one.start()
     for distance in (1, 2, 3):
-        near(distance, 0)
-        across(distance - 1, 0)
-        if distance == 2:
-            push(z, x, 2, (0, 1, 2, 4), own=True)
-            push(z, x, 1, (4,), own=True)
-    across(3, 0)
-    for distance in (1, 2, 3):
-        near(distance, 2)
-        across(distance - 1, 2)
-        mirrored(distance, x)
-        mirrored(distance - 1, 1 - x)
+        for kind in (0, 2):
+            near(distance, kind)
+        for kind in (0, 2):
+            across(distance - 1, kind)
+        if distance > 1:
+            mirrored(distance - 1, x)
+            mirrored(distance - 2, 1 - x)
+    for kind in (0, 2):
+        across(3, kind)
+    mirrored(3, x)
+    mirrored(2, 1 - x)
     mirrored(3, 1 - x)
-    across(3, 2)
     for zz in range(4):
         for xx in range(2):
             for kind in range(3):
@@ -246,16 +264,15 @@
         one.wait()
 
 
-def gather_all(normalized, prior, devices):
+def gather_all(normalized, lists, devices):
     rows, width = normalized.shape
-    classes = prior.shape[1]
     return pl.pallas_call(
         gather_kernel,
         in_specs=[pl.BlockSpec(memory_space=pl.ANY)] * 2,
         out_specs=[pl.BlockSpec(memory_space=pl.ANY)] * 2,
         out_shape=[
             jax.ShapeDtypeStruct((devices * rows, width), normalized.dtype),
-            jax.ShapeDtypeStruct((devices * rows, classes), prior.dtype),
+            jax.ShapeDtypeStruct((devices,) + lists.shape, lists.dtype),
         ],
         scratch_shapes=[
             pltpu.SemaphoreType.DMA((devices, 3)),
@@ -264,10 +281,10 @@
         ],
         compiler_params=pltpu.CompilerParams(collective_id=0, has_side_effects=True),
         cost_estimate=pl.CostEstimate(
-            flops=0, bytes_accessed=2 * devices * rows * (width + classes) * 2, transcendentals=0
+            flops=0, bytes_accessed=16 * devices * rows * width * 2, transcendentals=0
         ),
         name="gather",
-    )(normalized, prior)
+    )(normalized, lists)
 
 
 def on_device(features, class_bias, logits, tile_lists, valid_counts):
@@ -293,17 +310,18 @@
     splits = 1 if grid_links else 2
     part_width = prior.shape[1] // splits
     own_priors = [prior[:, s * part_width : (s + 1) * part_width] for s in range(splits)]
+    small = jnp.concatenate([tile_lists.reshape(-1), valid_counts])
+    listing = small.shape[0]
+    priors = [lax.all_gather(p, "dp", axis=0, tiled=True) for p in own_priors]
     if grid_links:
-        memory, gathered = gather_all(normalized, prior, devices)
-        priors = [gathered]
+        lists = jnp.pad(small, (0, 8 * 128 - listing)).reshape(8, 128)
+        memory, all_lists = gather_all(normalized, lists, devices)
+        small = all_lists.reshape(devices, -1)[:, :listing]
     else:
         share = own_rows // twins
         mine = lax.dynamic_slice_in_dim(normalized, twin * share, share, 0)
         memory = lax.all_gather(mine, ("dp", "tensor"), axis=0, tiled=True)
-        priors = [lax.all_gather(p, "dp", axis=0, tiled=True) for p in own_priors]
-
-    small = jnp.concatenate([tile_lists.reshape(-1), valid_counts])
-    small = lax.all_gather(small, "dp", axis=0, tiled=False)
+        small = lax.all_gather(small, "dp", axis=0, tiled=False)
     counts = small[:, -1]
     owners = small[:, :-1].reshape(-1)
     pairs = owners.reshape(-1, listed)
@@ -381,10 +399,6 @@
         name="weights",
     )(step_tile, slot_block, slot_first, used, counts, memory)
 
-    own_weights = weights.reshape(slots, block_rows, own_rows)[own_slot]
-    own_weights = own_weights.reshape(devices * capacity * block_rows, own_rows)
-    own_factor = lax.dynamic_slice_in_dim(factor, me * own_rows, own_rows, 0)
-
     def tile_of(step, tiles, *rest):
         return (tiles[step], 0)
 
@@ -393,6 +407,15 @@
 
     def same(*a):
         return (0, 0)
+
+    def own_at(j):
+        def place(step, tiles, sb, sf, n, ob, of, os, m):
+            return (os[jnp.maximum(step - chunks, 0) * capacity + j], 0)
+
+        return pl.BlockSpec((block_rows, own_rows), place)
+
+    def mine_at(step, tiles, sb, sf, n, ob, of, os, m):
+        return (m[0], 0)
 
     outs = []
     for piece, own_piece in zip(priors, own_priors):
@@ -400,15 +423,15 @@
             pl.pallas_call(
                 functools.partial(labels_kernel, chunks, block_rows, capacity),
                 grid_spec=pltpu.PrefetchScalarGridSpec(
-                    num_scalar_prefetch=7,
+                    num_scalar_prefetch=8,
                     grid=(chunks + devices,),
                     in_specs=[
                         pl.BlockSpec((GROUP * block_rows, own_rows), one_chunk),
-                        pl.BlockSpec((capacity * block_rows, own_rows), late_tile),
+                        *[own_at(j) for j in range(capacity)],
                         pl.BlockSpec((own_rows, part_width), tile_of),
                         pl.BlockSpec((own_rows, 128), late_tile),
                         pl.BlockSpec((own_rows, part_width), same),
-                        pl.BlockSpec((own_rows, 128), same),
+                        pl.BlockSpec((own_rows, 128), mine_at),
                     ],
                     out_specs=pl.BlockSpec((own_rows, part_width), same),
                     scratch_shapes=[
@@ -425,8 +448,8 @@
                 ),
                 name="labels",
             )(
-                step_tile, slot_block, slot_first, used, own_block, own_first, me.reshape(1),
-                weights, own_weights, piece, factor, own_piece, own_factor,
+                step_tile, slot_block, slot_first, used, own_block, own_first, own_slot,
+                me.reshape(1), weights, *[weights] * capacity, piece, factor, own_piece, factor,
             )
         )
     return outs[0] if splits == 1 else jnp.concatenate(outs, axis=1)

time: 284 us -> 294 us (1.035)
  Pallas kernels: 237 us -> 255 us
  between operations: 2.08 us -> 14.8 us
  local copies, waits for them, and re-layouts: 16.5 us -> 4.04 us
  blocking collectives: 14.5 us -> 4.38 us
    pallas_call x1, Pallas kernels: 134 us -> 149 us  [gather_all(): pl.pallas_call(gather_kernel, in_specs=[pl.BlockSpec(memory_space=pl.ANY)...]
    unnamed x1 -> x0, blocking collectives: 10.7 us -> none
    gather x1 -> x0, local copies, waits for them, and re-layouts: 10.1 us -> none  [on_device(): own_weights = weights.reshape(slots, block_rows, own_rows)[own_slot]]
  transfers between devices with their start and end apart: 0 -> 1, of which waited for: 0 -> 0; matrix products, arithmetic and copies ran while one was open for 0% -> 4% of each run, Pallas kernels for 0% -> 69%
where the time goes in v3:
time: 294 us; the launch traced here: 290 us
  Pallas kernels  255 us (87%)
  between operations  14.8 us (5%)
  other arithmetic  11.8 us (4%)
  blocking collectives  4.38 us (1%)
  local copies, waits for them, and re-layouts  4.04 us (1%)
    pallas_call x1, Pallas kernels, gather_all(): pl.pallas_call(gather_kernel, in_specs=[pl.BlockSpec(memory_space=pl.ANY)...  149 us
    pallas_call x1, Pallas kernels, on_device(): pl.pallas_call(functools.partial(labels_kernel, chunks, block_rows, capac...  56.1 us
    pallas_call x1, Pallas kernels, on_device(): pl.pallas_call(functools.partial(weights_kernel, block_rows, own_rows), g...  49.5 us
  transfers between devices with their start and end apart: 1, of which 0 were waited for; matrix products, arithmetic and copies ran while one was open for 4% of the time, Pallas kernels for 69%

profile of v3, /device:TPU:1, one launch (start us, length us, event | category | flops | bytes accessed | tf_op | source)
XLA Modules:
  0.0 289.8 jit_solution(1874315259033757814)
XLA Ops:
  6.5 0.0 all-gather.2.cloned.1.call-start
  6.5 1.6 fusion.3
  8.1 4.4 %psum.7 = f32[512]{0:T(512)S(1)} all-reduce(f32[512]{0:T(512)S(1)} %fusion.3), channel_id=1, replica_groups=mesh['dp'=16,'tensor'=2] {'tensor'}, use_global_device_ids=true, to_apply=%region_17.18 | all-reduce | flops 512 | bytes 4096 | tf_op jit(solution)/shard_map/psum | solution.py:307
  12.5 2.3 divide_convert_fusion.rest_6_
  14.8 0.0 all-gather.2.cloned.1.call-update
  15.5 0.1 copy.27
  15.6 0.1 reshape.150
  15.7 0.1 pad_add_fusion
  15.7 0.6 pad_bitcast_fusion.lists
  16.3 0.3 fusion
  16.7 1.4 fusion.2.features
  18.1 149.2 %gather.1 = (bf16[8192,1280]{1,0:T(8,128)(2,1)}, s32[16,8,128]{2,1,0:T(8,128)}) custom-call(bf16[512,1280]{1,0:T(8,128)(2,1)} %fusion.2.features, s32[8,128]{1,0:T(8,128)} %pad_bitcast_fusion.lists), custom_call_target="tpu_custom_call" | custom-call | bytes 335544320 | tf_op jit(solution)/shard_map/gather/pallas_call | solution.py:269
  167.3 0.9 copy.42
  168.2 0.1 eq.64
  168.2 1.1 reduce-window.10
  169.4 0.2 slice_reduce_fusion
  169.6 0.1 bitcast_bitcast_fusion
  169.7 0.2 fusion.12
  169.9 0.1 copy.29
  170.1 0.6 slice.44
  170.6 0.1 reduce.2
  170.7 0.1 eq.68
  170.8 0.1 reshape_reshape.3
  170.9 0.1 slice.47
  171.0 0.1 slice_compare_fusion.1
  171.1 0.1 copy.32
  171.2 0.1 copy.31
  171.3 0.1 copy.33
  171.5 0.1 reshape.156
  171.6 0.1 fusion.7
  171.7 0.1 reduce_window_sum.35
  171.7 0.2 fusion.10
  171.9 0.1 select_reduce_fusion.3
  172.0 0.1 dynamic_slice.7
  172.1 0.1 dynamic_slice.6
  172.2 0.6 copy.35
  173.4 0.1 convert_reduce_fusion
  173.5 0.6 pad_add_fusion.1.step_tile
  174.1 0.2 select_reduce_fusion.7
  174.3 0.1 fusion.6
  174.4 0.6 select_reduce_fusion.4
  175.0 0.2 fusion.4
  175.2 1.0 select_reduce_fusion
  176.2 0.5 broadcast_select_fusion.own_block
  176.7 0.6 fusion.14.slot_block
  177.3 49.5 %weights.1 = (bf16[24064,512]{1,0:T(8,128)(2,1)}, f32[8192,128]{1,0:T(8,128)}) custom-call(s32[63]{0:T(128)} %pad_add_fusion.1.step_tile, s32[752]{0:T(1024)} %fusion.14.slot_block, s32[752]{0:T(1024)} %get-tuple-element.13.slot_first, s32[1]{0:T(128)} %bitcast.4.used, s32[16]{0:T(128)} %bitcast.35, bf16[8192,1280]{1,0:T(8,128)(2,1)} %get-tuple-element.10.memory), custom_call_target="tpu_custom_call" | custom-call | flops 21474836480 | bytes 45613056 | tf_op jit(solution)/shard_map/weights/pallas_call | solution.py:373
  226.8 0.0 all-gather.2.cloned.1.call-done.rest_4_
  226.8 56.1 %labels.1 = f32[512,768]{1,0:T(8,128)} custom-call(s32[63]{0:T(128)} %pad_add_fusion.1.step_tile, s32[752]{0:T(1024)} %fusion.14.slot_block, s32[752]{0:T(1024)} %get-tuple-element.13.slot_first, s32[1]{0:T(128)} %bitcast.4.used, s32[64]{0:T(128)} %broadcast_select_fusion.own_block, s32[64]{0:T(128)} %get-tuple-element.18.own_first, ...), custom_call_target="tpu_custom_call" | custom-call | flops 12884901888 | bytes 24641536 | tf_op jit(solution)/shard_map/labels/pallas_call | solution.py:423
  (16 shorter events, 0.1 us)
Async XLA Ops:
  6.5 8.9 %copy-start.1 = (s32[16,2]{0,1:T(2,128)S(1)}, s32[16,2]{0,1:T(2,128)}, u32[]{:S(2)}) copy-start(s32[16,2]{0,1:T(2,128)} %param.8) | copy-start | bytes 388
  6.5 9.8 %copy-start = (bf16[512,1280]{1,0:T(8,128)(2,1)S(1)}, bf16[512,1280]{1,0:T(8,128)(2,1)}, u32[]{:S(2)}) copy-start(bf16[512,1280]{1,0:T(8,128)(2,1)} %param.5) | copy-start | bytes 3932164
  6.5 220.3 %all-gather.2.cloned.1.call-start = ((), (), s32[]{:S(2)}) async-start(), calls=%async_computation | async-start | bytes 13369344 | tf_op jit(solution)/shard_map/all_gather | solution.py:315
Sparse Core Ops, SparseCore 0:
  14.9 132.2 all-gather.1

commit v4 on v3

--- a/solution.py
+++ b/solution.py
@@ -43,9 +43,15 @@
         ]
         keys = held[pl.ds(pl.multiple_of(tile * tile_rows, tile_rows), tile_rows), :]
         some = GROUP // 2
+        where = [pl.ds(start, block_rows) for start in starts]
+        olds = [
+            jnp.where(slot_first[step * GROUP + j] == 1, 0.0, total[where[j], :])
+            for j in range(GROUP)
+        ]
+        news = []
         for begin in range(0, GROUP, some):
             queries = jnp.concatenate(
-                [held[pl.ds(s, block_rows), :] for s in starts[begin : begin + some]], axis=0
+                [held[rows_at, :] for rows_at in where[begin : begin + some]], axis=0
             )
             scores = lax.dot_general(
                 queries, keys, (((1,), (1,)), ((), ())), preferred_element_type=jnp.float32
@@ -56,11 +62,10 @@
             ).astype(jnp.bfloat16)
             out[begin * block_rows : (begin + some) * block_rows, :] = weights
             sums = jnp.sum(weights.astype(jnp.float32), axis=1, keepdims=True)
-            sums = jnp.broadcast_to(sums, (sums.shape[0], 128))
             for j in range(some):
-                where = pl.ds(starts[begin + j], block_rows)
-                old = jnp.where(slot_first[step * GROUP + begin + j] == 1, 0.0, total[where, :])
-                total[where, :] = old + sums[j * block_rows : (j + 1) * block_rows]
+                news.append(olds[begin + j] + sums[j * block_rows : (j + 1) * block_rows])
+        for j in range(GROUP):
+            total[where[j], :] = news[j]
 
     @pl.when(step == pl.num_programs(0) - 1)
     def _():
@@ -68,55 +73,64 @@
 
 
 def labels_kernel(
-    chunks, block_rows, own_slots, step_tile, slot_block, slot_first, used, own_block, own_first,
-    own_slot, me, weights, *rest
+    chunks, block_rows, own_slots, step_tile, position, used, own_slot, own_place, me, weights,
+    *rest
 ):
     own_weights = rest[:own_slots]
-    prior, factor, own_prior, own_factor, out, total, own_total = rest[own_slots:]
+    prior, factor, own_prior, own_factor, out, partial, own_partial = rest[own_slots:]
     step = pl.program_id(0)
     tile_rows, width = prior.shape
+    tile_blocks = tile_rows // block_rows
     piece = 256 if width % 256 == 0 else 128
     pieces = [slice(p, p + piece) for p in range(0, width, piece)]
 
-    def add(into, part, cut, blocks, firsts, base, number):
-        for j in range(number):
-            start = pl.multiple_of(blocks[base + j] * block_rows, block_rows)
-            where = pl.ds(start, block_rows)
-            old = jnp.where(firsts[base + j] == 1, 0.0, into[where, cut])
-            into[where, cut] = old + part[j * block_rows : (j + 1) * block_rows]
+    def summed(source, places, base, cut):
+        found = []
+        for j in range(tile_blocks):
+            pair = [
+                source[pl.ds(pl.multiple_of(places[base + 2 * j + k] * block_rows, block_rows),
+                             block_rows), cut].astype(jnp.float32)
+                for k in range(2)
+            ]
+            found.append(pair[0] + pair[1])
+        return jnp.concatenate(found, axis=0)
 
     def wide(lanes):
         return jnp.concatenate([lanes] * (piece // 128), axis=1)
 
     @pl.when(step < used[0])
     def _():
+        size = weights.shape[0]
+        rows = pl.ds(pl.multiple_of(step * size, size), size)
         for cut in pieces:
             part = jnp.dot(weights[...], prior[:, cut], preferred_element_type=jnp.float32)
-            add(total, part, cut, slot_block, slot_first, step * GROUP, GROUP)
+            partial[rows, cut] = part.astype(jnp.bfloat16)
 
     @pl.when(step >= chunks)
     def _():
         tile = step - chunks
-        rows = pl.ds(pl.multiple_of(tile * tile_rows, tile_rows), tile_rows)
+        size = own_slots * block_rows
+        rows = pl.ds(pl.multiple_of(tile * size, size), size)
         sent = jnp.concatenate([w[...] for w in own_weights], axis=0)
         scale = wide(factor[...])
         for cut in pieces:
-            labels = total[rows, cut] * scale + (1.0 - ALPHA) * prior[:, cut].astype(jnp.float32)
+            numerator = summed(partial, position, tile * tile_blocks * 2, cut)
+            labels = numerator * scale + (1.0 - ALPHA) * prior[:, cut].astype(jnp.float32)
             part = jnp.dot(
                 sent, labels.astype(jnp.bfloat16), preferred_element_type=jnp.float32
             )
-            add(own_total, part, cut, own_block, own_first, tile * own_slots, own_slots)
+            own_partial[rows, cut] = part.astype(jnp.bfloat16)
 
     @pl.when(step == pl.num_programs(0) - 1)
     def _():
         scale = wide(own_factor[...])
         for cut in pieces:
-            spread = own_total[pl.ds(0, tile_rows), cut] * scale
+            spread = summed(own_partial, own_place, 0, cut) * scale
             spread += (1.0 - ALPHA) * own_prior[:, cut].astype(jnp.float32)
             out[:, cut] = jnp.log(spread)
 
 
-def gather_kernel(features, lists, memory, all_lists, recv, send, local):
+def gather_kernel(features, labels, lists, memory, priors, all_lists, recv, send, local):
     dp, y = lax.axis_index("dp"), lax.axis_index("tensor")
     z, x, c = dp // 4, (dp // 2) % 2, dp % 2
     rows = features.shape[0]
@@ -126,14 +140,18 @@
         return zz * 4 + xx * 2 + c
 
     def region(t, kind):
+        if kind == 3:
+            return all_lists.at[t]
         if kind == 2:
-            return all_lists.at[t]
+            return priors.at[pl.ds(pl.multiple_of(t * rows, rows), rows)]
         h = y if kind == 0 else 1 - y
         return memory.at[pl.ds(pl.multiple_of(t * rows + h * half, half), half)]
 
     def own_region(kind):
+        if kind == 3:
+            return lists
         if kind == 2:
-            return lists
+            return labels
         h = y if kind == 0 else 1 - y
         return features.at[pl.ds(pl.multiple_of(h * half, half), half)]
 
@@ -227,31 +245,35 @@
     pl.semaphore_wait(barrier, 4 + z * (3 - z) // 2)
 
     push(z, x, 0, (0, 1, 2, 4), own=True)
-    push(z, x, 2, (0, 1, 2, 4), own=True)
-    push(z, x, 1, (4,), own=True)
+    push(z, x, 3, (0, 1, 2, 4), own=True)
     keep = pl.ds(pl.multiple_of(dp * rows, rows), rows)
     copies = [
         pltpu.make_async_copy(features, memory.at[keep], local.at[0]),
-        pltpu.make_async_copy(lists, all_lists.at[dp], local.at[1]),
+        pltpu.make_async_copy(labels, priors.at[keep], local.at[1]),
+        pltpu.make_async_copy(lists, all_lists.at[dp], local.at[2]),
     ]
     for one in copies:
         one.start()
     for distance in (1, 2, 3):
-        for kind in (0, 2):
-            near(distance, kind)
-        for kind in (0, 2):
-            across(distance - 1, kind)
-        if distance > 1:
-            mirrored(distance - 1, x)
-            mirrored(distance - 2, 1 - x)
-    for kind in (0, 2):
-        across(3, kind)
-    mirrored(3, x)
-    mirrored(2, 1 - x)
+        near(distance, 0)
+        across(distance - 1, 0)
+        near(distance, 3)
+        across(distance - 1, 3)
+        if distance == 2:
+            push(z, x, 2, (0, 1, 2, 4), own=True)
+            push(z, x, 1, (4,), own=True)
+    across(3, 0)
+    across(3, 3)
+    for distance in (1, 2, 3):
+        near(distance, 2)
+        across(distance - 1, 2)
+        mirrored(distance, x)
+        mirrored(distance - 1, 1 - x)
     mirrored(3, 1 - x)
+    across(3, 2)
     for zz in range(4):
         for xx in range(2):
-            for kind in range(3):
+            for kind in range(4):
                 landed(zz * 4 + xx * 2 + 1 - c, kind)
     for guards, zz, xx, kind, way, own in sent:
         guarded(
@@ -264,27 +286,29 @@
         one.wait()
 
 
-def gather_all(normalized, lists, devices):
+def gather_all(normalized, prior, lists, devices):
     rows, width = normalized.shape
+    classes = prior.shape[1]
     return pl.pallas_call(
         gather_kernel,
-        in_specs=[pl.BlockSpec(memory_space=pl.ANY)] * 2,
-        out_specs=[pl.BlockSpec(memory_space=pl.ANY)] * 2,
+        in_specs=[pl.BlockSpec(memory_space=pl.ANY)] * 3,
+        out_specs=[pl.BlockSpec(memory_space=pl.ANY)] * 3,
         out_shape=[
             jax.ShapeDtypeStruct((devices * rows, width), normalized.dtype),
+            jax.ShapeDtypeStruct((devices * rows, classes), prior.dtype),
             jax.ShapeDtypeStruct((devices,) + lists.shape, lists.dtype),
         ],
         scratch_shapes=[
-            pltpu.SemaphoreType.DMA((devices, 3)),
-            pltpu.SemaphoreType.DMA((8, 3, 5)),
-            pltpu.SemaphoreType.DMA((2,)),
+            pltpu.SemaphoreType.DMA((devices, 4)),
+            pltpu.SemaphoreType.DMA((8, 4, 5)),
+            pltpu.SemaphoreType.DMA((3,)),
         ],
         compiler_params=pltpu.CompilerParams(collective_id=0, has_side_effects=True),
         cost_estimate=pl.CostEstimate(
-            flops=0, bytes_accessed=16 * devices * rows * width * 2, transcendentals=0
+            flops=0, bytes_accessed=2 * devices * rows * (width + classes) * 2, transcendentals=0
         ),
         name="gather",
-    )(normalized, lists)
+    )(normalized, prior, lists)
 
 
 def on_device(features, class_bias, logits, tile_lists, valid_counts):
@@ -312,16 +336,17 @@
     own_priors = [prior[:, s * part_width : (s + 1) * part_width] for s in range(splits)]
     small = jnp.concatenate([tile_lists.reshape(-1), valid_counts])
     listing = small.shape[0]
-    priors = [lax.all_gather(p, "dp", axis=0, tiled=True) for p in own_priors]
     if grid_links:
         lists = jnp.pad(small, (0, 8 * 128 - listing)).reshape(8, 128)
-        memory, all_lists = gather_all(normalized, lists, devices)
+        memory, gathered, all_lists = gather_all(normalized, prior, lists, devices)
+        priors = [gathered]
         small = all_lists.reshape(devices, -1)[:, :listing]
     else:
         share = own_rows // twins
         mine = lax.dynamic_slice_in_dim(normalized, twin * share, share, 0)
         memory = lax.all_gather(mine, ("dp", "tensor"), axis=0, tiled=True)
         small = lax.all_gather(small, "dp", axis=0, tiled=False)
+        priors = [lax.all_gather(p, "dp", axis=0, tiled=True) for p in own_priors]
     counts = small[:, -1]
     owners = small[:, :-1].reshape(-1)
     pairs = owners.reshape(-1, listed)
@@ -356,16 +381,11 @@
     own_matches = (
         own_place[None, :] == jnp.arange(devices * capacity, dtype=jnp.int32)[:, None]
     )
-    own_filled = jnp.any(own_matches, axis=1)
 
     def placed(values):
         return jnp.sum(jnp.where(own_matches, values[None, :], 0), axis=1)
 
-    own_first = placed(lax.dynamic_slice_in_dim(firsts, me * own_requests, own_requests))
     own_slot = placed(lax.dynamic_slice_in_dim(position, me * own_requests, own_requests))
-    own_block = jnp.where(
-        own_filled, placed(jnp.arange(own_requests, dtype=jnp.int32) // listed), block_count
-    )
 
     def one_chunk(step, tiles, sb, sf, n, *rest):
         return (jnp.minimum(step, n[0] - 1), 0)
@@ -408,13 +428,16 @@
     def same(*a):
         return (0, 0)
 
+    def used_chunk(step, tiles, ps, n, *rest):
+        return (jnp.minimum(step, n[0] - 1), 0)
+
     def own_at(j):
-        def place(step, tiles, sb, sf, n, ob, of, os, m):
+        def place(step, tiles, ps, n, os, op, m):
             return (os[jnp.maximum(step - chunks, 0) * capacity + j], 0)
 
         return pl.BlockSpec((block_rows, own_rows), place)
 
-    def mine_at(step, tiles, sb, sf, n, ob, of, os, m):
+    def mine_at(step, tiles, ps, n, os, op, m):
         return (m[0], 0)
 
     outs = []
@@ -423,10 +446,10 @@
             pl.pallas_call(
                 functools.partial(labels_kernel, chunks, block_rows, capacity),
                 grid_spec=pltpu.PrefetchScalarGridSpec(
-                    num_scalar_prefetch=8,
+                    num_scalar_prefetch=6,
                     grid=(chunks + devices,),
                     in_specs=[
-                        pl.BlockSpec((GROUP * block_rows, own_rows), one_chunk),
+                        pl.BlockSpec((GROUP * block_rows, own_rows), used_chunk),
                         *[own_at(j) for j in range(capacity)],
                         pl.BlockSpec((own_rows, part_width), tile_of),
                         pl.BlockSpec((own_rows, 128), late_tile),
@@ -435,8 +458,10 @@
                     ],
                     out_specs=pl.BlockSpec((own_rows, part_width), same),
                     scratch_shapes=[
-                        pltpu.VMEM((rows + block_rows, part_width), jnp.float32),
-                        pltpu.VMEM((own_rows + block_rows, part_width), jnp.float32),
+                        pltpu.VMEM((slots * block_rows, part_width), jnp.bfloat16),
+                        pltpu.VMEM(
+                            (devices * capacity * block_rows, part_width), jnp.bfloat16
+                        ),
                     ],
                 ),
                 out_shape=jax.ShapeDtypeStruct((own_rows, part_width), jnp.float32),
@@ -448,8 +473,8 @@
                 ),
                 name="labels",
             )(
-                step_tile, slot_block, slot_first, used, own_block, own_first, own_slot,
-                me.reshape(1), weights, *[weights] * capacity, piece, factor, own_piece, factor,
+                step_tile, position, used, own_slot, own_place, me.reshape(1), weights, *[weights] * capacity,
+                piece, factor, own_piece, factor,
             )
         )
     return outs[0] if splits == 1 else jnp.concatenate(outs, axis=1)

time: 294 us -> 261 us (0.89); the launches traced: 290 us -> 263 us
  Pallas kernels: 255 us -> 241 us
  between operations: 14.8 us -> 1.42 us
    pallas_call x1, Pallas kernels: 149 us -> 135 us  [gather_all(): pl.pallas_call(gather_kernel, in_specs=[pl.BlockSpec(memory_space=pl.ANY)...]
  transfers between devices with their start and end apart: 1 -> 0, of which waited for: 0 -> 0; matrix products, arithmetic and copies ran while one was open for 4% -> 0% of each run, Pallas kernels for 69% -> 0%
where the time goes in v4:
time: 261 us; the launch traced here: 263 us
  Pallas kernels  241 us (92%)
  other arithmetic  11.1 us (4%)
  local copies, waits for them, and re-layouts  4.71 us (2%)
  blocking collectives  4.38 us (2%)
    pallas_call x1, Pallas kernels, gather_all(): pl.pallas_call(gather_kernel, in_specs=[pl.BlockSpec(memory_space=pl.ANY)...  135 us
    pallas_call x1, Pallas kernels, on_device(): pl.pallas_call(functools.partial(labels_kernel, chunks, block_rows, capac...  56.1 us
    pallas_call x1, Pallas kernels, on_device(): pl.pallas_call(functools.partial(weights_kernel, block_rows, own_rows), g...  50.4 us

profile of v4, /device:TPU:1, one launch (start us, length us, event | category | flops | bytes accessed | tf_op | source)
XLA Modules:
  0.0 262.8 jit_solution(2466458232872478110)
XLA Ops:
  0.0 0.0 copy-start
  0.0 0.9 copy.27
  0.9 0.1 reshape.136
  1.6 0.1 pad_add_fusion
  1.7 0.6 pad_bitcast_fusion.lists
  2.3 1.5 fusion.3
  3.7 4.4 %psum.7 = f32[512]{0:T(512)S(1)} all-reduce(f32[512]{0:T(512)S(1)} %fusion.3), channel_id=1, replica_groups=mesh['dp'=16,'tensor'=2] {'tensor'}, use_global_device_ids=true, to_apply=%region_2.0 | all-reduce | flops 512 | bytes 4096 | tf_op jit(solution)/shard_map/psum | solution.py:331
  8.1 2.3 divide_convert_fusion.labels.rest_6_
  10.4 0.0 copy-done
  10.4 0.3 fusion
  10.8 1.4 fusion.2.features
  12.2 134.7 %gather.1 = (bf16[8192,1280]{1,0:T(8,128)(2,1)}, bf16[8192,768]{1,0:T(8,128)(2,1)}, s32[16,8,128]{2,1,0:T(8,128)}) custom-call(bf16[512,1280]{1,0:T(8,128)(2,1)} %fusion.2.features, bf16[512,768]{1,0:T(8,128)(2,1)} %divide_convert_fusion.labels.rest_6_, s32[8,128]{1,0:T(8,128)} %pad_bitcast_fusion.lists), custom_call_target="tpu_custom_call" | custom-call | bytes 67108864 | tf_op jit(solution)/shard_map/gather/pallas_call | solution.py:292
  146.9 0.9 copy.42
  147.7 0.1 eq.64
  147.8 1.1 reduce-window.10
  149.0 0.2 slice_reduce_fusion
  149.2 0.1 bitcast_bitcast_fusion
  149.3 0.2 fusion.11
  149.5 0.1 copy.29
  149.6 0.2 fusion.9
  149.8 0.1 eq.68
  149.9 0.1 select_reduce_fusion.3
  150.0 0.0 copy-start.1
  150.0 0.1 reshape_reshape.3
  150.1 0.1 slice_compare_fusion.1
  150.3 0.1 copy.31
  150.3 0.1 copy.32
  150.5 0.1 copy.33
  150.6 0.1 reshape.142
  150.8 1.0 select_reduce_fusion
  151.7 0.2 fusion.4
  152.0 0.6 fusion.13.slot_block
  152.6 0.5 slice.44
  153.7 0.1 reduce.2
  153.9 0.1 convert_reduce_fusion
  153.9 0.6 pad_add_fusion.1.step_tile
  154.6 0.1 slice.47
  154.6 0.6 copy.35
  155.2 50.4 %weights.1 = (bf16[24064,512]{1,0:T(8,128)(2,1)}, f32[8192,128]{1,0:T(8,128)}) custom-call(s32[63]{0:T(128)} %pad_add_fusion.1.step_tile, s32[752]{0:T(1024)} %fusion.13.slot_block, s32[752]{0:T(1024)} %get-tuple-element.15.slot_first, s32[1]{0:T(128)} %bitcast.4.used, s32[16]{0:T(128)} %bitcast.35, bf16[8192,1280]{1,0:T(8,128)(2,1)} %get-tuple-element.11.memory), custom_call_target="tpu_custom_call" | custom-call | flops 21474836480 | bytes 45613056 | tf_op jit(solution)/shard_map/weights/pallas_call | solution.py:393
  205.7 0.0 copy-done.1
  205.7 0.1 dynamic_slice.3
  205.7 0.1 fusion.6
  205.8 0.1 reduce_window_sum.35
  205.9 0.2 select_reduce_fusion.5
  206.1 0.0 copy-start.2
  206.1 0.6 select_reduce_fusion.4.own_slot
  206.7 0.0 copy-done.2
  206.7 56.1 %labels.1 = f32[512,768]{1,0:T(8,128)} custom-call(s32[63]{0:T(128)} %pad_add_fusion.1.step_tile, s32[512]{0:T(512)} %copy-done.1, s32[1]{0:T(128)} %bitcast.4.used, s32[64]{0:T(128)} %select_reduce_fusion.4.own_slot, s32[32]{0:T(128)} %copy-done.2, s32[1]{0:T(128)} %bitcast.5.me, ...), custom_call_target="tpu_custom_call" | custom-call | flops 12884901888 | bytes 24641536 | tf_op jit(solution)/shard_map/labels/pallas_call | solution.py:446
  (12 shorter events, 0.1 us)
Async XLA Ops:
  0.0 10.4 %copy-start = (bf16[512,1280]{1,0:T(8,128)(2,1)S(1)}, bf16[512,1280]{1,0:T(8,128)(2,1)}, u32[]{:S(2)}) copy-start(bf16[512,1280]{1,0:T(8,128)(2,1)} %param.5) | copy-start | bytes 3932164
  150.0 55.6 %copy-start.1 = (s32[512]{0:T(512)}, s32[512]{0:T(512)S(1)}, u32[]{:S(2)}) copy-start(s32[512]{0:T(512)S(1)} %multiply_add_fusion.position) | copy-start | bytes 6148
  206.1 0.6 copy-start.2

commit v5 on v4

--- a/solution.py
+++ b/solution.py
@@ -73,13 +73,15 @@
 
 
 def labels_kernel(
-    chunks, block_rows, own_slots, step_tile, position, used, own_slot, own_place, me, weights,
-    *rest
+    chunks, block_rows, own_slots, step_tile, position, used, own_slot, own_place, me,
+    all_weights, all_priors, factor, own_factor, out, partial, own_partial, own_weights, prior,
+    ring, sem, prior_sems, ring_sems
 ):
-    own_weights = rest[:own_slots]
-    prior, factor, own_prior, own_factor, out, partial, own_partial = rest[own_slots:]
     step = pl.program_id(0)
-    tile_rows, width = prior.shape
+    tile_rows, width = out.shape
+    tiles = prior.shape[0] // tile_rows
+    size = ring.shape[1]
+    depth = ring.shape[0]
     tile_blocks = tile_rows // block_rows
     piece = 256 if width % 256 == 0 else 128
     pieces = [slice(p, p + piece) for p in range(0, width, piece)]
@@ -98,24 +100,87 @@
     def wide(lanes):
         return jnp.concatenate([lanes] * (piece // 128), axis=1)
 
+    def prior_rows(tile):
+        return pl.ds(pl.multiple_of(tile * tile_rows, tile_rows), tile_rows)
+
+    def prior_copy(tile):
+        return pltpu.make_async_copy(
+            all_priors.at[prior_rows(tile)], prior.at[prior_rows(tile)], prior_sems.at[tile]
+        )
+
+    def ring_copy(chunk):
+        return pltpu.make_async_copy(
+            all_weights.at[pl.ds(pl.multiple_of(chunk * size, size), size)],
+            ring.at[chunk % depth],
+            ring_sems.at[chunk % depth],
+        )
+
+    def fetch(chunk):
+        @pl.when(chunk < used[0])
+        def _():
+            ring_copy(chunk).start()
+
+    @pl.when(step == 0)
+    def _():
+        fetch(0)
+
+        @pl.loop(0, tiles)
+        def _(tile):
+            prior_copy(tile).start()
+
+        for chunk in range(1, depth - 1):
+            fetch(chunk)
+
+        @pl.loop(0, own_weights.shape[0] // block_rows)
+        def _(i):
+            start = pl.multiple_of(own_slot[i] * block_rows, block_rows)
+            pltpu.make_async_copy(
+                all_weights.at[pl.ds(start, block_rows)],
+                own_weights.at[pl.ds(pl.multiple_of(i * block_rows, block_rows), block_rows)],
+                sem,
+            ).start()
+
+    before = jnp.where(step == 0, -1, step_tile[jnp.maximum(step - 1, 0)])
+
+    @pl.when(step == chunks)
+    def _():
+        pltpu.make_async_copy(
+            all_weights.at[pl.ds(0, own_weights.shape[0])], own_weights, sem
+        ).wait()
+
+        @pl.loop(before + 1, tiles)
+        def _(tile):
+            prior_copy(tile).wait()
+
     @pl.when(step < used[0])
     def _():
-        size = weights.shape[0]
+        fetch(step + depth - 1)
+
+        @pl.loop(before + 1, step_tile[step] + 1)
+        def _(tile):
+            prior_copy(tile).wait()
+
+        ring_copy(step).wait()
         rows = pl.ds(pl.multiple_of(step * size, size), size)
+        weights = ring[step % depth]
         for cut in pieces:
-            part = jnp.dot(weights[...], prior[:, cut], preferred_element_type=jnp.float32)
+            part = jnp.dot(
+                weights, prior[prior_rows(step_tile[step]), cut],
+                preferred_element_type=jnp.float32,
+            )
             partial[rows, cut] = part.astype(jnp.bfloat16)
 
     @pl.when(step >= chunks)
     def _():
         tile = step - chunks
-        size = own_slots * block_rows
-        rows = pl.ds(pl.multiple_of(tile * size, size), size)
-        sent = jnp.concatenate([w[...] for w in own_weights], axis=0)
+        count = own_slots * block_rows
+        rows = pl.ds(pl.multiple_of(tile * count, count), count)
+        sent = own_weights[rows, :]
         scale = wide(factor[...])
         for cut in pieces:
             numerator = summed(partial, position, tile * tile_blocks * 2, cut)
-            labels = numerator * scale + (1.0 - ALPHA) * prior[:, cut].astype(jnp.float32)
+            labels = numerator * scale
+            labels += (1.0 - ALPHA) * prior[prior_rows(tile), cut].astype(jnp.float32)
             part = jnp.dot(
                 sent, labels.astype(jnp.bfloat16), preferred_element_type=jnp.float32
             )
@@ -126,11 +191,14 @@
         scale = wide(own_factor[...])
         for cut in pieces:
             spread = summed(own_partial, own_place, 0, cut) * scale
-            spread += (1.0 - ALPHA) * own_prior[:, cut].astype(jnp.float32)
+            spread += (1.0 - ALPHA) * prior[prior_rows(me[0]), cut].astype(jnp.float32)
             out[:, cut] = jnp.log(spread)
 
 
-def gather_kernel(features, labels, lists, memory, priors, all_lists, recv, send, local):
+def gather_kernel(
+    features, logits, bias, lists, memory, priors, all_lists, labels, raised, sums, twin_sums,
+    recv, send, local, sums_sent, sums_came
+):
     dp, y = lax.axis_index("dp"), lax.axis_index("tensor")
     z, x, c = dp // 4, (dp // 2) % 2, dp % 2
     rows = features.shape[0]
@@ -249,11 +317,35 @@
     keep = pl.ds(pl.multiple_of(dp * rows, rows), rows)
     copies = [
         pltpu.make_async_copy(features, memory.at[keep], local.at[0]),
-        pltpu.make_async_copy(labels, priors.at[keep], local.at[1]),
-        pltpu.make_async_copy(lists, all_lists.at[dp], local.at[2]),
+        pltpu.make_async_copy(lists, all_lists.at[dp], local.at[1]),
+        pltpu.make_async_copy(labels, priors.at[keep], local.at[2]),
     ]
-    for one in copies:
+    for one in copies[:2]:
         one.start()
+    slab = 64
+
+    @pl.loop(0, rows // slab)
+    def _(i):
+        at = pl.ds(pl.multiple_of(i * slab, slab), slab)
+        grown = jnp.exp(logits[at, :].astype(jnp.float32) + bias[...])
+        raised[at, :] = grown
+        sums[at, :] = jnp.broadcast_to(jnp.sum(grown, axis=1, keepdims=True), (slab, 128))
+
+    swap = pltpu.make_async_remote_copy(
+        src_ref=sums, dst_ref=twin_sums, send_sem=sums_sent, recv_sem=sums_came,
+        device_id=partner(3), device_id_type=pl.DeviceIdType.MESH,
+    )
+    swap.start()
+    swap.wait()
+
+    @pl.loop(0, rows // slab)
+    def _(i):
+        at = pl.ds(pl.multiple_of(i * slab, slab), slab)
+        whole = sums[at, :] + twin_sums[at, :]
+        whole = jnp.concatenate([whole] * (raised.shape[1] // 128), axis=1)
+        labels[at, :] = (raised[at, :] / whole).astype(jnp.bfloat16)
+
+    copies[2].start()
     for distance in (1, 2, 3):
         near(distance, 0)
         across(distance - 1, 0)
@@ -286,29 +378,42 @@
         one.wait()
 
 
-def gather_all(normalized, prior, lists, devices):
+def gather_all(normalized, logits, bias, lists, devices):
     rows, width = normalized.shape
-    classes = prior.shape[1]
+    classes = logits.shape[1]
     return pl.pallas_call(
         gather_kernel,
-        in_specs=[pl.BlockSpec(memory_space=pl.ANY)] * 3,
+        in_specs=[
+            pl.BlockSpec(memory_space=pl.ANY),
+            pl.BlockSpec(memory_space=pltpu.VMEM),
+            pl.BlockSpec(memory_space=pltpu.VMEM),
+            pl.BlockSpec(memory_space=pl.ANY),
+        ],
         out_specs=[pl.BlockSpec(memory_space=pl.ANY)] * 3,
         out_shape=[
             jax.ShapeDtypeStruct((devices * rows, width), normalized.dtype),
-            jax.ShapeDtypeStruct((devices * rows, classes), prior.dtype),
+            jax.ShapeDtypeStruct((devices * rows, classes), jnp.bfloat16),
             jax.ShapeDtypeStruct((devices,) + lists.shape, lists.dtype),
         ],
         scratch_shapes=[
+            pltpu.VMEM((rows, classes), jnp.bfloat16),
+            pltpu.VMEM((rows, classes), jnp.float32),
+            pltpu.VMEM((rows, 128), jnp.float32),
+            pltpu.VMEM((rows, 128), jnp.float32),
             pltpu.SemaphoreType.DMA((devices, 4)),
             pltpu.SemaphoreType.DMA((8, 4, 5)),
             pltpu.SemaphoreType.DMA((3,)),
+            pltpu.SemaphoreType.DMA,
+            pltpu.SemaphoreType.DMA,
         ],
-        compiler_params=pltpu.CompilerParams(collective_id=0, has_side_effects=True),
+        compiler_params=pltpu.CompilerParams(
+            collective_id=0, has_side_effects=True, vmem_limit_bytes=VMEM_BYTES // 3
+        ),
         cost_estimate=pl.CostEstimate(
             flops=0, bytes_accessed=2 * devices * rows * (width + classes) * 2, transcendentals=0
         ),
         name="gather",
-    )(normalized, prior, lists)
+    )(normalized, logits, bias, lists)
 
 
 def on_device(features, class_bias, logits, tile_lists, valid_counts):
@@ -326,22 +431,24 @@
     twin = lax.axis_index("tensor")
 
     normalized = unitnorm_rows(features)
-    adjusted = logits.astype(jnp.float32) + class_bias[None, :]
-    exponentials = jnp.exp(adjusted)
-    row_totals = lax.psum(jnp.sum(exponentials, axis=1), "tensor")
-    prior = (exponentials / row_totals[:, None]).astype(jnp.bfloat16)
     grid_links = devices == 16 and twins == 2
     splits = 1 if grid_links else 2
-    part_width = prior.shape[1] // splits
-    own_priors = [prior[:, s * part_width : (s + 1) * part_width] for s in range(splits)]
+    part_width = logits.shape[1] // splits
     small = jnp.concatenate([tile_lists.reshape(-1), valid_counts])
     listing = small.shape[0]
     if grid_links:
         lists = jnp.pad(small, (0, 8 * 128 - listing)).reshape(8, 128)
-        memory, gathered, all_lists = gather_all(normalized, prior, lists, devices)
+        memory, gathered, all_lists = gather_all(
+            normalized, logits, class_bias[None, :], lists, devices
+        )
         priors = [gathered]
         small = all_lists.reshape(devices, -1)[:, :listing]
     else:
+        adjusted = logits.astype(jnp.float32) + class_bias[None, :]
+        exponentials = jnp.exp(adjusted)
+        row_totals = lax.psum(jnp.sum(exponentials, axis=1), "tensor")
+        prior = (exponentials / row_totals[:, None]).astype(jnp.bfloat16)
+        own_priors = [prior[:, s * part_width : (s + 1) * part_width] for s in range(splits)]
         share = own_rows // twins
         mine = lax.dynamic_slice_in_dim(normalized, twin * share, share, 0)
         memory = lax.all_gather(mine, ("dp", "tensor"), axis=0, tiled=True)
@@ -419,29 +526,17 @@
         name="weights",
     )(step_tile, slot_block, slot_first, used, counts, memory)
 
-    def tile_of(step, tiles, *rest):
-        return (tiles[step], 0)
-
     def late_tile(step, *rest):
         return (jnp.maximum(step - chunks, 0), 0)
 
     def same(*a):
         return (0, 0)
 
-    def used_chunk(step, tiles, ps, n, *rest):
-        return (jnp.minimum(step, n[0] - 1), 0)
-
-    def own_at(j):
-        def place(step, tiles, ps, n, os, op, m):
-            return (os[jnp.maximum(step - chunks, 0) * capacity + j], 0)
-
-        return pl.BlockSpec((block_rows, own_rows), place)
-
     def mine_at(step, tiles, ps, n, os, op, m):
         return (m[0], 0)
 
     outs = []
-    for piece, own_piece in zip(priors, own_priors):
+    for piece in priors:
         outs.append(
             pl.pallas_call(
                 functools.partial(labels_kernel, chunks, block_rows, capacity),
@@ -449,19 +544,27 @@
                     num_scalar_prefetch=6,
                     grid=(chunks + devices,),
                     in_specs=[
-                        pl.BlockSpec((GROUP * block_rows, own_rows), used_chunk),
-                        *[own_at(j) for j in range(capacity)],
-                        pl.BlockSpec((own_rows, part_width), tile_of),
+                        pl.BlockSpec(memory_space=pl.ANY),
+                        pl.BlockSpec(memory_space=pl.ANY),
                         pl.BlockSpec((own_rows, 128), late_tile),
-                        pl.BlockSpec((own_rows, part_width), same),
-                        pl.BlockSpec((own_rows, 128), mine_at),
+                        pl.BlockSpec(
+                            (own_rows, 128), mine_at, pipeline_mode=pl.Buffered(1)
+                        ),
                     ],
-                    out_specs=pl.BlockSpec((own_rows, part_width), same),
+                    out_specs=pl.BlockSpec(
+                        (own_rows, part_width), same, pipeline_mode=pl.Buffered(1)
+                    ),
                     scratch_shapes=[
                         pltpu.VMEM((slots * block_rows, part_width), jnp.bfloat16),
                         pltpu.VMEM(
                             (devices * capacity * block_rows, part_width), jnp.bfloat16
                         ),
+                        pltpu.VMEM((devices * capacity * block_rows, own_rows), jnp.bfloat16),
+                        pltpu.VMEM((rows, part_width), jnp.bfloat16),
+                        pltpu.VMEM((4, GROUP * block_rows, own_rows), jnp.bfloat16),
+                        pltpu.SemaphoreType.DMA,
+                        pltpu.SemaphoreType.DMA((devices,)),
+                        pltpu.SemaphoreType.DMA((4,)),
                     ],
                 ),
                 out_shape=jax.ShapeDtypeStruct((own_rows, part_width), jnp.float32),
@@ -473,8 +576,8 @@
                 ),
                 name="labels",
             )(
-                step_tile, position, used, own_slot, own_place, me.reshape(1), weights, *[weights] * capacity,
-                piece, factor, own_piece, factor,
+                step_tile, position, used, own_slot, own_place, me.reshape(1), weights, piece, factor,
+                factor,
             )
         )
     return outs[0] if splits == 1 else jnp.concatenate(outs, axis=1)

time: 261 us -> 251 us (0.962)
  Pallas kernels: 241 us -> 233 us
  blocking collectives: 4.38 us -> 0 us
  local copies, waits for them, and re-layouts: 4.71 us -> 8.49 us
  other arithmetic: 11.1 us -> 7.57 us
    pallas_call x1, Pallas kernels: 56.1 us -> 46.4 us  [on_device(): pl.pallas_call(functools.partial(labels_kernel, chunks, block_rows, capac...]
    psum x1 -> x0, blocking collectives: 4.38 us -> none  [on_device(): row_totals = lax.psum(jnp.sum(exponentials, axis=1), 'tensor')]
    unnamed x9 -> x15, local copies, waits for them, and re-layouts: 2.31 us -> 6.66 us
where the time goes in v5:
time: 251 us
  Pallas kernels  233 us (93%)
  local copies, waits for them, and re-layouts  8.49 us (3%)
  other arithmetic  7.57 us (3%)
    pallas_call x1, Pallas kernels, gather_all(): pl.pallas_call(gather_kernel, in_specs=[pl.BlockSpec(memory_space=pl.ANY)...  135 us
    pallas_call x1, Pallas kernels, on_device(): pl.pallas_call(functools.partial(weights_kernel, block_rows, own_rows), g...  51.4 us
    pallas_call x1, Pallas kernels, on_device(): pl.pallas_call(functools.partial(labels_kernel, chunks, block_rows, capac...  46.4 us
    unnamed x15, local copies, waits for them, and re-layouts  6.66 us

profile of v5, /device:TPU:1, one launch (start us, length us, event | category | flops | bytes accessed | tf_op | source)
XLA Modules:
  0.0 250.8 jit_solution(1649592407525778034)
XLA Ops:
  0.0 0.9 copy.27
  0.9 0.1 reshape.134
  1.6 0.1 pad_add_fusion
  1.7 1.6 fusion
  3.3 0.0 copy-start.4
  3.3 0.0 copy-start
  3.4 0.0 copy-done.2
  3.4 0.4 fusion.2.features
  3.8 0.3 copy-done.4
  4.0 0.5 copy-done
  4.5 135.4 %gather.1 = (bf16[8192,1280]{1,0:T(8,128)(2,1)}, bf16[8192,768]{1,0:T(8,128)(2,1)S(1)}, s32[16,8,128]{2,1,0:T(8,128)S(1)}) custom-call(bf16[512,1280]{1,0:T(8,128)(2,1)S(1)} %fusion.2.features, bf16[512,768]{1,0:T(8,128)(2,1)S(1)} %copy-done, f32[1,768]{1,0:T(1,128)S(1)} %broadcast_in_dim.50.bias, s32[8,128]{1,0:T(8,128)S(1)} %pad_bitcast_fusion.lists), custom_call_target="tpu_custom_call" | custom-call | bytes 67108864 | tf_op jit(solution)/shard_map/gather/pallas_call | solution.py:384
  139.9 0.0 copy-start.1
  139.9 4.5 %copy-done.1 = bf16[8192,768]{1,0:T(8,128)(2,1)} copy-done((bf16[8192,768]{1,0:T(8,128)(2,1)}, bf16[8192,768]{1,0:T(8,128)(2,1)S(1)}, u32[]{:S(2)}) %copy-start.1) | copy-done | bytes 12582936
  144.4 0.1 eq.64
  144.5 1.1 reduce-window.10
  145.6 0.2 slice_reduce_fusion
  145.9 0.1 bitcast_bitcast_fusion
  146.0 0.2 fusion.10
  146.2 0.1 copy.29
  146.3 0.2 fusion.8
  146.5 0.1 eq.68
  146.6 0.1 select_reduce_fusion.3
  146.7 0.0 copy-start.3
  146.7 0.1 reshape_reshape.3
  146.8 0.1 slice_compare_fusion.1
  146.9 0.1 copy.31
  147.0 0.1 copy.32
  147.1 0.1 copy.33
  147.3 0.1 reshape.140
  147.4 1.0 select_reduce_fusion
  148.4 0.2 fusion.3
  148.6 0.6 fusion.12.slot_block
  149.2 0.5 slice.44
  150.4 0.1 reduce.2
  150.5 0.1 convert_reduce_fusion
  150.6 0.6 pad_add_fusion.1.step_tile
  151.2 0.1 slice.47
  151.3 0.6 copy.35
  151.9 51.4 %weights.1 = (bf16[24064,512]{1,0:T(8,128)(2,1)}, f32[8192,128]{1,0:T(8,128)}) custom-call(s32[63]{0:T(128)} %pad_add_fusion.1.step_tile, s32[752]{0:T(1024)} %fusion.12.slot_block, s32[752]{0:T(1024)} %get-tuple-element.15.slot_first, s32[1]{0:T(128)} %bitcast.4.used, s32[16]{0:T(128)} %bitcast.35, bf16[8192,1280]{1,0:T(8,128)(2,1)} %get-tuple-element.11.memory), custom_call_target="tpu_custom_call" | custom-call | flops 21474836480 | bytes 45613056 | tf_op jit(solution)/shard_map/weights/pallas_call | solution.py:500
  203.3 0.0 copy-done.3
  203.3 0.1 dynamic_slice.3
  203.4 0.1 fusion.5
  203.5 0.1 reduce_window_sum.35
  203.5 0.2 select_reduce_fusion.5
  203.7 0.0 copy-start.5
  203.7 0.6 select_reduce_fusion.4.own_slot
  204.4 0.0 copy-done.5
  204.4 46.4 %labels.1 = f32[512,768]{1,0:T(8,128)} custom-call(s32[63]{0:T(128)} %pad_add_fusion.1.step_tile, s32[512]{0:T(512)} %copy-done.3, s32[1]{0:T(128)} %bitcast.4.used, s32[64]{0:T(128)} %select_reduce_fusion.4.own_slot, s32[32]{0:T(128)} %copy-done.5, s32[1]{0:T(128)} %bitcast.5.me, bf16[24064,512]{1,0:T(8,128)(2,1)} %get-tuple-element.12.all_weights, ...), custom_call_target="tpu_custom_call" | custom-call | flops 12884901888 | bytes 24641536 | tf_op jit(solution)/shard_map/labels/pallas_call | solution.py:541
  (16 shorter events, 0.2 us)
Async XLA Ops:
  0.0 3.4 %copy-start.2 = (bf16[512,1280]{1,0:T(8,128)(2,1)S(1)}, bf16[512,1280]{1,0:T(8,128)(2,1)}, u32[]{:S(2)}) copy-start(bf16[512,1280]{1,0:T(8,128)(2,1)} %param.5) | copy-start | bytes 3932164
  3.3 0.7 copy-start.4
  3.3 1.1 copy-start
  139.9 4.5 %copy-start.1 = (bf16[8192,768]{1,0:T(8,128)(2,1)}, bf16[8192,768]{1,0:T(8,128)(2,1)S(1)}, u32[]{:S(2)}) copy-start(bf16[8192,768]{1,0:T(8,128)(2,1)S(1)} %get-tuple-element.13.all_priors) | copy-start | bytes 37748740
  146.7 56.6 %copy-start.3 = (s32[512]{0:T(512)}, s32[512]{0:T(512)S(1)}, u32[]{:S(2)}) copy-start(s32[512]{0:T(512)S(1)} %multiply_add_fusion.position) | copy-start | bytes 6148
  203.7 0.6 copy-start.5

commit v6 on v5

--- a/solution.py
+++ b/solution.py
@@ -265,9 +265,9 @@
             device_id_type=pl.DeviceIdType.MESH,
         )
 
-    def push(zz, xx, kind, ways, exists=None, own=False):
+    def push(zz, xx, kind, ways, exists=None, own=False, skip_across=None):
         for way in ways:
-            guards = (exists, reach(way))
+            guards = (exists, reach(way), skip_across if way == 2 else None)
             guarded(guards, lambda way=way: copy(zz, xx, kind, way, own).start())
             sent.append((guards, zz, xx, kind, way, own))
 
@@ -290,12 +290,16 @@
         for zz, exists, ways in column(distance):
             guarded((exists,), lambda zz=zz: landed(index(zz, x), kind))
             onward = ways + ((2, 3, 4) if kind == 0 else (2, 4))
-            push(zz, x, kind, onward, exists)
+            paired = zz != z + 1 - 2 * (z % 2) if kind == 2 and distance == 1 else None
+            push(zz, x, kind, onward, exists, skip_across=paired)
 
     def across(distance, kind):
         for zz, exists, _ in column(distance):
             guarded((exists,), lambda zz=zz: landed(index(zz, 1 - x), kind))
             push(zz, 1 - x, kind, (3, 4) if kind == 0 else (4,), exists)
+            if kind == 2 and distance == 0:
+                push(zz, 1 - x, kind, (1,), z % 2 == 0)
+                push(zz, 1 - x, kind, (0,), z % 2 == 1)
 
     def mirrored(distance, xx):
         for zz, exists, _ in column(distance):
@@ -407,7 +411,7 @@
             pltpu.SemaphoreType.DMA,
         ],
         compiler_params=pltpu.CompilerParams(
-            collective_id=0, has_side_effects=True, vmem_limit_bytes=VMEM_BYTES // 3
+            collective_id=0, has_side_effects=True, vmem_limit_bytes=VMEM_BYTES
         ),
         cost_estimate=pl.CostEstimate(
             flops=0, bytes_accessed=2 * devices * rows * (width + classes) * 2, transcendentals=0

time: 251 us -> 246 us (0.980)
  local copies, waits for them, and re-layouts: 8.49 us -> 5.32 us
  Pallas kernels: 233 us -> 230 us
    unnamed x15 -> x11, local copies, waits for them, and re-layouts: 6.66 us -> 2.31 us
    pallas_call x1, Pallas kernels: 51.4 us -> 47.4 us  [on_device(): pl.pallas_call(functools.partial(weights_kernel, block_rows, own_rows), g...]
    pallas_call x1, Pallas kernels: 135 us -> 139 us  [gather_all(): pl.pallas_call(gather_kernel, in_specs=[pl.BlockSpec(memory_space=pl.ANY)...]
where the time goes in v6:
time: 246 us
  Pallas kernels  230 us (93%)
  other arithmetic  8.63 us (4%)
  local copies, waits for them, and re-layouts  5.32 us (2%)
    pallas_call x1, Pallas kernels, gather_all(): pl.pallas_call(gather_kernel, in_specs=[pl.BlockSpec(memory_space=pl.ANY)...  139 us
    pallas_call x1, Pallas kernels, on_device(): pl.pallas_call(functools.partial(weights_kernel, block_rows, own_rows), g...  47.4 us
    pallas_call x1, Pallas kernels, on_device(): pl.pallas_call(functools.partial(labels_kernel, chunks, block_rows, capac...  44.1 us

profile of v6, /device:TPU:1, one launch (start us, length us, event | category | flops | bytes accessed | tf_op | source)
XLA Modules:
  0.0 245.9 jit_solution(9587396419020978895)
XLA Ops:
  0.0 0.0 copy-start
  0.0 0.9 copy.27
  0.9 0.1 reshape.134
  1.6 0.1 pad_add_fusion
  1.7 0.6 pad_bitcast_fusion.lists
  2.3 1.6 fusion
  3.9 0.0 copy-start.2
  3.9 0.0 copy-done
  4.0 1.4 fusion.2.features
  5.4 0.0 copy-done.2
  5.4 0.6 broadcast_in_dim.50.bias
  6.0 139.0 %gather.1 = (bf16[8192,1280]{1,0:T(8,128)(2,1)}, bf16[8192,768]{1,0:T(8,128)(2,1)}, s32[16,8,128]{2,1,0:T(8,128)}) custom-call(bf16[512,1280]{1,0:T(8,128)(2,1)} %fusion.2.features, bf16[512,768]{1,0:T(8,128)(2,1)} %logits.1, f32[1,768]{1,0:T(1,128)} %broadcast_in_dim.50.bias, s32[8,128]{1,0:T(8,128)} %pad_bitcast_fusion.lists), custom_call_target="tpu_custom_call" | custom-call | bytes 67108864 | tf_op jit(solution)/shard_map/gather/pallas_call | solution.py:388
  145.0 0.9 copy.42
  145.8 0.1 eq.64
  145.9 1.1 reduce-window.10
  147.1 0.2 slice_reduce_fusion
  147.3 0.1 bitcast_bitcast_fusion
  147.4 0.2 fusion.10
  147.6 0.1 copy.29
  147.7 0.2 fusion.8
  147.9 0.1 eq.68
  148.0 0.1 select_reduce_fusion.3
  148.1 0.0 copy-start.1
  148.1 0.1 reshape_reshape.3
  148.2 0.1 slice_compare_fusion.1
  148.4 0.1 copy.31
  148.4 0.1 copy.32
  148.6 0.1 copy.33
  148.7 0.1 reshape.140
  148.9 1.0 select_reduce_fusion
  149.8 0.2 fusion.3
  150.1 0.6 fusion.12.slot_block
  150.7 0.5 slice.44
  151.8 0.1 reduce.2
  152.0 0.1 convert_reduce_fusion
  152.1 0.6 pad_add_fusion.1.step_tile
  152.7 0.1 slice.47
  152.7 0.6 copy.35
  153.3 47.4 %weights.1 = (bf16[24064,512]{1,0:T(8,128)(2,1)}, f32[8192,128]{1,0:T(8,128)}) custom-call(s32[63]{0:T(128)} %pad_add_fusion.1.step_tile, s32[752]{0:T(1024)} %fusion.12.slot_block, s32[752]{0:T(1024)} %get-tuple-element.15.slot_first, s32[1]{0:T(128)} %bitcast.4.used, s32[16]{0:T(128)} %bitcast.35, bf16[8192,1280]{1,0:T(8,128)(2,1)} %get-tuple-element.11.memory), custom_call_target="tpu_custom_call" | custom-call | flops 21474836480 | bytes 45613056 | tf_op jit(solution)/shard_map/weights/pallas_call | solution.py:504
  200.8 0.0 copy-done.1
  200.8 0.1 dynamic_slice.3
  200.8 0.1 fusion.5
  200.9 0.1 reduce_window_sum.35
  201.0 0.2 select_reduce_fusion.5
  201.2 0.0 copy-start.3
  201.2 0.6 select_reduce_fusion.4.own_slot
  201.8 0.0 copy-done.3
  201.8 44.1 %labels.1 = f32[512,768]{1,0:T(8,128)} custom-call(s32[63]{0:T(128)} %pad_add_fusion.1.step_tile, s32[512]{0:T(512)} %copy-done.1, s32[1]{0:T(128)} %bitcast.4.used, s32[64]{0:T(128)} %select_reduce_fusion.4.own_slot, s32[32]{0:T(128)} %copy-done.3, s32[1]{0:T(128)} %bitcast.5.me, bf16[24064,512]{1,0:T(8,128)(2,1)} %get-tuple-element.12.all_weights, ...), custom_call_target="tpu_custom_call" | custom-call | flops 12884901888 | bytes 24641536 | tf_op jit(solution)/shard_map/labels/pallas_call | solution.py:545
  (12 shorter events, 0.1 us)
Async XLA Ops:
  0.0 3.9 %copy-start = (bf16[512,1280]{1,0:T(8,128)(2,1)S(1)}, bf16[512,1280]{1,0:T(8,128)(2,1)}, u32[]{:S(2)}) copy-start(bf16[512,1280]{1,0:T(8,128)(2,1)} %param.5) | copy-start | bytes 3932164
  3.9 1.5 copy-start.2
  148.1 52.6 %copy-start.1 = (s32[512]{0:T(512)}, s32[512]{0:T(512)S(1)}, u32[]{:S(2)}) copy-start(s32[512]{0:T(512)S(1)} %multiply_add_fusion.position) | copy-start | bytes 6148
  201.2 0.6 copy-start.3

commit v7 on v6

--- a/solution.py
+++ b/solution.py
@@ -290,7 +290,9 @@
         for zz, exists, ways in column(distance):
             guarded((exists,), lambda zz=zz: landed(index(zz, x), kind))
             onward = ways + ((2, 3, 4) if kind == 0 else (2, 4))
-            paired = zz != z + 1 - 2 * (z % 2) if kind == 2 and distance == 1 else None
+            paired = None
+            if kind == 2 and distance == 1:
+                paired = jnp.logical_or(zz != z + 1 - 2 * (z % 2), z % 3 == 0)
             push(zz, x, kind, onward, exists, skip_across=paired)
 
     def across(distance, kind):
@@ -298,8 +300,8 @@
             guarded((exists,), lambda zz=zz: landed(index(zz, 1 - x), kind))
             push(zz, 1 - x, kind, (3, 4) if kind == 0 else (4,), exists)
             if kind == 2 and distance == 0:
-                push(zz, 1 - x, kind, (1,), z % 2 == 0)
-                push(zz, 1 - x, kind, (0,), z % 2 == 1)
+                push(zz, 1 - x, kind, (1,), z == 0)
+                push(zz, 1 - x, kind, (0,), z == 3)
 
     def mirrored(distance, xx):
         for zz, exists, _ in column(distance):
@@ -355,7 +357,7 @@
         across(distance - 1, 0)
         near(distance, 3)
         across(distance - 1, 3)
-        if distance == 2:
+        if distance == 1:
             push(z, x, 2, (0, 1, 2, 4), own=True)
             push(z, x, 1, (4,), own=True)
     across(3, 0)

time: 246 us -> 247 us (level)
  Pallas kernels: 230 us -> 234 us
    pallas_call x1, Pallas kernels: 47.4 us -> 50.4 us  [on_device(): pl.pallas_call(functools.partial(weights_kernel, block_rows, own_rows), g...]
where the time goes in v7:
time: 247 us; the launch traced here: 249 us
  Pallas kernels  234 us (95%)
  other arithmetic  8.63 us (3%)
  local copies, waits for them, and re-layouts  5.32 us (2%)
    pallas_call x1, Pallas kernels, gather_all(): pl.pallas_call(gather_kernel, in_specs=[pl.BlockSpec(memory_space=pl.ANY)...  137 us
    pallas_call x1, Pallas kernels, on_device(): pl.pallas_call(functools.partial(weights_kernel, block_rows, own_rows), g...  50.4 us
    pallas_call x1, Pallas kernels, on_device(): pl.pallas_call(functools.partial(labels_kernel, chunks, block_rows, capac...  45.9 us

profile of v7, /device:TPU:1, one launch (start us, length us, event | category | flops | bytes accessed | tf_op | source)
XLA Modules:
  0.0 248.9 jit_solution(5783273657312797062)
XLA Ops:
  0.0 0.0 copy-start
  0.0 0.9 copy.27
  0.9 0.1 reshape.134
  1.6 0.1 pad_add_fusion
  1.7 0.6 pad_bitcast_fusion.lists
  2.3 1.6 fusion
  3.9 0.0 copy-start.2
  3.9 0.0 copy-done
  4.0 1.4 fusion.2.features
  5.4 0.0 copy-done.2
  5.4 0.6 broadcast_in_dim.50.bias
  6.0 137.2 %gather.1 = (bf16[8192,1280]{1,0:T(8,128)(2,1)}, bf16[8192,768]{1,0:T(8,128)(2,1)}, s32[16,8,128]{2,1,0:T(8,128)}) custom-call(bf16[512,1280]{1,0:T(8,128)(2,1)} %fusion.2.features, bf16[512,768]{1,0:T(8,128)(2,1)} %logits.1, f32[1,768]{1,0:T(1,128)} %broadcast_in_dim.50.bias, s32[8,128]{1,0:T(8,128)} %pad_bitcast_fusion.lists), custom_call_target="tpu_custom_call" | custom-call | bytes 67108864 | tf_op jit(solution)/shard_map/gather/pallas_call | solution.py:390
  143.2 0.9 copy.42
  144.1 0.1 eq.64
  144.2 1.1 reduce-window.10
  145.3 0.2 slice_reduce_fusion
  145.6 0.1 bitcast_bitcast_fusion
  145.6 0.2 fusion.10
  145.9 0.1 copy.29
  146.0 0.2 fusion.8
  146.2 0.1 eq.68
  146.3 0.1 select_reduce_fusion.3
  146.4 0.0 copy-start.1
  146.4 0.1 reshape_reshape.3
  146.5 0.1 slice_compare_fusion.1
  146.6 0.1 copy.31
  146.7 0.1 copy.32
  146.8 0.1 copy.33
  147.0 0.1 reshape.140
  147.1 1.0 select_reduce_fusion
  148.1 0.2 fusion.3
  148.3 0.6 fusion.12.slot_block
  148.9 0.5 slice.44
  150.1 0.1 reduce.2
  150.2 0.1 convert_reduce_fusion
  150.3 0.6 pad_add_fusion.1.step_tile
  150.9 0.1 slice.47
  151.0 0.6 copy.35
  151.6 50.4 %weights.1 = (bf16[24064,512]{1,0:T(8,128)(2,1)}, f32[8192,128]{1,0:T(8,128)}) custom-call(s32[63]{0:T(128)} %pad_add_fusion.1.step_tile, s32[752]{0:T(1024)} %fusion.12.slot_block, s32[752]{0:T(1024)} %get-tuple-element.15.slot_first, s32[1]{0:T(128)} %bitcast.4.used, s32[16]{0:T(128)} %bitcast.35, bf16[8192,1280]{1,0:T(8,128)(2,1)} %get-tuple-element.11.memory), custom_call_target="tpu_custom_call" | custom-call | flops 21474836480 | bytes 45613056 | tf_op jit(solution)/shard_map/weights/pallas_call | solution.py:506
  202.0 0.0 copy-done.1
  202.0 0.1 dynamic_slice.3
  202.1 0.1 fusion.5
  202.2 0.1 reduce_window_sum.35
  202.2 0.2 select_reduce_fusion.5
  202.4 0.0 copy-start.3
  202.4 0.6 select_reduce_fusion.4.own_slot
  203.1 0.0 copy-done.3
  203.1 45.9 %labels.1 = f32[512,768]{1,0:T(8,128)} custom-call(s32[63]{0:T(128)} %pad_add_fusion.1.step_tile, s32[512]{0:T(512)} %copy-done.1, s32[1]{0:T(128)} %bitcast.4.used, s32[64]{0:T(128)} %select_reduce_fusion.4.own_slot, s32[32]{0:T(128)} %copy-done.3, s32[1]{0:T(128)} %bitcast.5.me, bf16[24064,512]{1,0:T(8,128)(2,1)} %get-tuple-element.12.all_weights, ...), custom_call_target="tpu_custom_call" | custom-call | flops 12884901888 | bytes 24641536 | tf_op jit(solution)/shard_map/labels/pallas_call | solution.py:547
  (12 shorter events, 0.1 us)
Async XLA Ops:
  0.0 3.9 %copy-start = (bf16[512,1280]{1,0:T(8,128)(2,1)S(1)}, bf16[512,1280]{1,0:T(8,128)(2,1)}, u32[]{:S(2)}) copy-start(bf16[512,1280]{1,0:T(8,128)(2,1)} %param.5) | copy-start | bytes 3932164
  3.9 1.5 copy-start.2
  146.4 55.6 %copy-start.1 = (s32[512]{0:T(512)}, s32[512]{0:T(512)S(1)}, u32[]{:S(2)}) copy-start(s32[512]{0:T(512)S(1)} %multiply_add_fusion.position) | copy-start | bytes 6148
  202.4 0.6 copy-start.3
